TPU v7x, 256 devices: a whole 4x4x8 slice. The times are simulated.
256 devices in a mesh: lat: 64 (over y, z, x_hi), lon: 4 (over x_lo, core).
Axes of the slice: x: 4 (x_hi: 2, x_lo: 2; x = x_hi * 2 + x_lo), y: 4, z: 8, core: 2. Of those that a mesh axis runs over, the one named last changes fastest.
Arguments:
- features: bfloat16 [256, 128, 512], P(None, 'lat', 'lon'), may hold values from -6 to 6
- weight: bfloat16 [256, 2304], replicated, may hold values from -0.125 to 0.125
- filter_table: float32 [16, 9, 5], replicated, may hold values from -1.2 to 1.2
- row_range: int32 [128, 2], replicated, may hold values from 0 to 5, as said below
- basis_id: int32 [128, 5], replicated, may hold values from 0 to 15
- cotangent: bfloat16 [256, 128, 512], P(None, 'lat', 'lon'), may hold values from -6 to 6
Outputs:
- output: bfloat16 [256, 128, 512], P(None, 'lat', 'lon')
- input_grad: bfloat16 [256, 128, 512], P(None, 'lat', 'lon')
- weight_grad: float32 [256, 2304], replicated
Inputs may be any that keep to these rules, and one draw needn't show every extreme that they name: `row_range`: column 0 never exceeds 2 and column 1 always exceeds 2; the first and last 2 rows use the whole window.
All inputs are finite; a program needn't handle non-finite values.
Results may differ from a plain program's by a relative error of at most 0.0059.
Values may be sent and summed in bfloat16 or wider, within the bound.
A program may use at most 128 MiB of HBM per device.

v0:
```python
import math

import jax
import jax.numpy as jnp
from jax import lax
from jax.sharding import PartitionSpec as P

H = 2
LH = 2


def padded(cells, sides, width, closed):
    for axis, dim in sides:
        count = lax.axis_size(axis)
        ends = count if closed else count - 1
        head = lax.slice_in_dim(cells, 0, width, axis=dim)
        tail = lax.slice_in_dim(cells, cells.shape[dim] - width, cells.shape[dim], axis=dim)
        cells = jnp.concatenate(
            [
                lax.ppermute(tail, axis, [(i, (i + 1) % count) for i in range(ends)]),
                cells,
                lax.ppermute(head, axis, [((i + 1) % count, i) for i in range(ends)]),
            ],
            axis=dim,
        )
    return cells


def from_behind(block, axis, distance):
    devices = range(lax.axis_size(axis))
    route = [(i - distance, i) for i in devices if i - distance in devices]
    return lax.ppermute(block, axis, route)


def passed_along(value, axis, steps):
    count = lax.axis_size(axis)
    pairs = [(source, (source + steps) % count) for source in range(count)]
    return lax.ppermute(value, axis, pairs)


def band_coef(filter_table, row_range, basis_id, start_row, count):
    shapes = filter_table.shape[0]
    reach = (basis_id.shape[1] - 1) // 2
    ids_pad = jnp.pad(basis_id, ((reach, reach), (0, 0)))
    range_pad = jnp.pad(row_range, ((reach, reach), (0, 0)))
    band_ids = lax.dynamic_slice_in_dim(ids_pad, start_row + reach, count, 0)
    band_range = lax.dynamic_slice_in_dim(range_pad, start_row + reach, count, 0)
    onehot = (band_ids[:, :, None] == jnp.arange(shapes, dtype=jnp.int32)[None, None, :]).astype(
        jnp.float32
    )
    lookup = jnp.einsum("tjb,bkl->tkjl", onehot, filter_table, precision=lax.Precision.HIGHEST)
    offsets = jnp.arange(basis_id.shape[1], dtype=jnp.int32)
    active = (offsets[None, :] >= band_range[:, 0:1]) & (offsets[None, :] < band_range[:, 1:2])
    return (lookup * active[:, None, :, None].astype(jnp.float32)).astype(jnp.bfloat16)


def per_device(features, weight, filter_table, row_range, basis_id, cotangent):
    channels, band_rows, lon_cols = features.shape
    out_channels = weight.shape[0]
    kernels = filter_table.shape[1]
    window = basis_id.shape[1]
    taps = filter_table.shape[2]
    n_lat = lax.axis_size("lat")
    n_lon = lax.axis_size("lon")
    first_row = lax.axis_index("lat") * band_rows
    filter_coef = band_coef(filter_table, row_range, basis_id, first_row, band_rows)
    rim_rows = padded(features, (("lat", 1),), H, False)
    extended = padded(rim_rows, (("lon", 2),), LH, True)
    basis_list = []
    for i in range(band_rows):
        stacked = jnp.stack(
            [extended[:, i + j, l : l + lon_cols] for j in range(window) for l in range(taps)],
            axis=1,
        )
        row_coef = filter_coef[i].reshape(kernels, window * taps)
        basis_list.append(
            jnp.einsum("cmp,km->ckp", stacked, row_coef, preferred_element_type=jnp.float32).astype(
                jnp.bfloat16
            )
        )
    basis_out = jnp.stack(basis_list, axis=2).reshape(channels * kernels, band_rows * lon_cols)
    output = (
        jnp.dot(weight, basis_out, preferred_element_type=jnp.float32)
        .astype(jnp.bfloat16)
        .reshape(out_channels, band_rows, lon_cols)
    )
    flat_cot = cotangent.reshape(out_channels, band_rows * lon_cols)
    local_grad = lax.dot_general(
        flat_cot, basis_out, (((1,), (1,)), ((), ())), preferred_element_type=jnp.float32
    )
    grad_sum = lax.psum(local_grad, ("lat", "lon"))
    weight_grad = grad_sum * jnp.float32(1.0 / math.sqrt(band_rows * n_lat * lon_cols * n_lon))
    basis_grad = lax.dot_general(
        weight, flat_cot, (((0,), (0,)), ((), ())), preferred_element_type=jnp.float32
    )
    basis_grad = basis_grad.astype(jnp.bfloat16).reshape(channels, kernels, band_rows, lon_cols)
    ext_list = [
        jnp.zeros((channels, lon_cols + 2 * LH), jnp.float32) for e in range(band_rows + 2 * H)
    ]
    for i in range(band_rows):
        for j in range(window):
            mixed = jnp.einsum(
                "ckp,kl->clp",
                basis_grad[:, :, i],
                filter_coef[i, :, j, :],
                preferred_element_type=jnp.float32,
            )
            for l in range(taps):
                ext_list[i + j] = ext_list[i + j] + jnp.pad(mixed[:, l], ((0, 0), (l, 2 * LH - l)))
    ext_sum = jnp.stack(ext_list, axis=1)
    top_rim = ext_sum[:, :H]
    bottom_rim = ext_sum[:, H + band_rows :]
    middle = ext_sum[:, H : H + band_rows]
    from_next = from_behind(top_rim, "lat", -1)
    from_prev = from_behind(bottom_rim, "lat", 1)
    middle = middle.at[:, :H].add(from_prev)
    middle = middle.at[:, band_rows - H :].add(from_next)
    left_edge = middle[:, :, :LH]
    right_edge = middle[:, :, LH + lon_cols :]
    center = middle[:, :, LH : LH + lon_cols]
    from_right = passed_along(left_edge, "lon", -1)
    from_left = passed_along(right_edge, "lon", 1)
    center = center.at[:, :, lon_cols - LH :].add(from_right)
    center = center.at[:, :, :LH].add(from_left)
    input_grad = center.astype(jnp.bfloat16)
    return (output, input_grad, weight_grad)


def solution(mesh):
    in_specs = (P(None, "lat", "lon"), P(), P(), P(), P(), P(None, "lat", "lon"))
    out_specs = (P(None, "lat", "lon"), P(None, "lat", "lon"), P())
    return jax.shard_map(
        per_device, mesh=mesh, in_specs=in_specs, out_specs=out_specs, check_vma=False
    )
```

profile of v0, /device:TPU:1, one launch (start us, length us, event | category | flops | bytes accessed | tf_op | source)
XLA Modules:
  0.0 380.2 jit_solution(13842729928420212777)
XLA Ops:
  7.2 6.3 %collective-permute-start = (bf16[256,2,128]{2,1,0:T(2,128)(2,1)}, bf16[256,2,128]{2,1,0:T(2,128)(2,1)}, u32[]{:S(2)}, u32[]{:S(2)}) collective-permute-start(bf16[256,2,128]{2,1,0:T(2,128)(2,1)} %param.18), channel_id=1, source_target_pairs={{0,4},{4,8},{8,12},{12,16},{16,20},{20,24},{24,28},{28,32},{32,36}... | collective-permute-start | bytes 393224 | tf_op jit(solution)/shard_map/ppermute | solution.py:20
  13.5 1.3 collective-permute-start.1
  16.4 0.9 copy.108
  18.2 1.4 convolution_convert_fusion
  20.0 1.6 fusion.50
  25.9 6.3 %collective-permute-start.4 = (f32[256,2,132]{2,0,1:T(8,128)}, f32[256,2,132]{2,0,1:T(8,128)}, u32[]{:S(2)}, u32[]{:S(2)}) collective-permute-start(f32[256,2,132]{2,0,1:T(8,128)} %pad_maximum_fusion.3), channel_id=1, source_target_pairs={{0,4},{4,8},{8,12},{12,16},{16,20},{20,24},{24,28},{28,32},{32,36}... | collective-permute-start | bytes 811016 | tf_op jit(solution)/shard_map/ppermute | solution.py:32
  36.5 1.5 collective-permute-start.5
  38.0 0.9 fusion.58
  41.1 1.3 add_bitcast_fusion.5
  42.5 1.3 add_bitcast_fusion.4
  43.8 1.4 pad_maximum_fusion.2
  45.4 1.8 collective-permute-start.2
  47.2 1.9 fusion.56
  49.2 1.9 fusion.57
  51.1 12.9 %collective-permute-done.2 = bf16[256,6,2]{2,1,0:T(8,128)(2,1)S(1)} collective-permute-done((bf16[256,6,2]{2,1,0:T(8,128)(2,1)S(1)}, bf16[256,6,2]{2,1,0:T(8,128)(2,1)S(1)}, u32[]{:S(2)}, u32[]{:S(2)}) %collective-permute-start.2) | collective-permute-done | bytes 6176 | tf_op jit(solution)/shard_map/ppermute | solution.py:20
  64.0 2.5 collective-permute-done.3
  66.5 3.2 pad_maximum_fusion.1
  69.8 2.8 fusion.53
  72.5 3.5 fusion.52
  76.0 10.7 %stack.40 = bf16[256,25,128]{2,1,0:T(8,128)(2,1)S(1)} concatenate(bf16[256,1,128]{2,1,0:T(2,128)(2,1)} %get-tuple-element.109, bf16[256,1,128]{2,1,0:T(2,128)(2,1)} %get-tuple-element.98, bf16[256,1,128]{2,1,0:T(2,128)(2,1)} %get-tuple-element.161, bf16[256,1,128]{2,1,0:T(2,128)(2,1)} %get-tuple-element.97, bf16[256,1,128]{2,1,0:T(2,128)(2,1)} %get-tuple-element.86, ...), dimensions={1} | concatenate | bytes 3276800 | tf_op jit(solution)/shard_map/stack | solution.py:71
  86.7 1.4 fusion
  88.1 10.6 %stack.42 = bf16[256,25,128]{2,1,0:T(8,128)(2,1)S(1)} concatenate(bf16[256,1,128]{2,1,0:T(2,128)(2,1)} %get-tuple-element.108, bf16[256,1,128]{2,1,0:T(2,128)(2,1)} %get-tuple-element.107, bf16[256,1,128]{2,1,0:T(2,128)(2,1)} %get-tuple-element.162, bf16[256,1,128]{2,1,0:T(2,128)(2,1)} %get-tuple-element.96, bf16[256,1,128]{2,1,0:T(2,128)(2,1)} %get-tuple-element.95, ...), dimensions={1} | concatenate | bytes 3276800 | tf_op jit(solution)/shard_map/stack | solution.py:71
  100.4 1.8 copy.113
  102.3 1.9 convolution_bitcast_fusion
  104.2 0.9 copy-done.3
  105.2 1.3 fusion.12
  108.7 1.8 collective-permute-start.7
  110.5 3.6 collective-permute-done.6
  114.2 1.2 scatter-add.6
  116.9 252.7 %all-reduce.54.cloned.1.call-done = f32[256,2304]{0,1:T(8,128)} async-done(((f32[256,2304]{0,1:T(8,128)}), f32[256,2304]{0,1:T(8,128)}) %all-reduce.54.cloned.1.call-update) | async-done | bytes 2359312 | tf_op jit(solution)/shard_map/psum | solution.py:91
  369.6 1.8 broadcast_multiply_fusion
  371.4 2.0 copy.131
  (93 shorter events, 19.2 us)
Async XLA Ops:
  7.2 11.1 %copy-start = (bf16[256,2304]{1,0:T(8,128)(2,1)S(1)}, bf16[256,2304]{1,0:T(8,128)(2,1)}, u32[]{:S(2)}) copy-start(bf16[256,2304]{1,0:T(8,128)(2,1)} %param.19) | copy-start | bytes 3538948
  7.2 362.4 %all-reduce.54.cloned.1.call-start = ((), (), s32[]{:S(2)}) async-start(), calls=%async_computation | async-start | bytes 4718592 | tf_op jit(solution)/shard_map/psum | solution.py:91
  7.2 36.5 %collective-permute-start = (bf16[256,2,128]{2,1,0:T(2,128)(2,1)}, bf16[256,2,128]{2,1,0:T(2,128)(2,1)}, u32[]{:S(2)}, u32[]{:S(2)}) collective-permute-start(bf16[256,2,128]{2,1,0:T(2,128)(2,1)} %param.18), channel_id=1, source_target_pairs={{0,4},{4,8},{8,12},{12,16},{16,20},{20,24},{24,28},{28,32},{32,36}... | collective-permute-start | bytes 393224 | tf_op jit(solution)/shard_map/ppermute | solution.py:20
  13.5 30.3 %collective-permute-start.1 = (bf16[256,2,128]{2,1,0:T(2,128)(2,1)}, bf16[256,2,128]{2,1,0:T(2,128)(2,1)}, u32[]{:S(2)}, u32[]{:S(2)}) collective-permute-start(bf16[256,2,128]{2,1,0:T(2,128)(2,1)} %param.18), channel_id=1, source_target_pairs={{4,0},{8,4},{12,8},{16,12},{20,16},{24,20},{28,24},{32,28},{36,32}... | collective-permute-start | bytes 393224 | tf_op jit(solution)/shard_map/ppermute | solution.py:22
  17.6 0.6 copy-start.6
  20.0 1.7 copy-start.13
  21.9 0.7 copy-start.12
  22.9 0.7 copy-start.11
  24.4 7.7 %copy-start.10 = (bf16[1,9,1,5]{1,2,3,0:T(2,128)(2,1)S(1)}, bf16[1,9,1,5]{1,2,3,0:T(2,128)(2,1)}, u32[]{:S(2)}) copy-start(bf16[1,9,1,5]{1,2,3,0:T(2,128)(2,1)} %get-tuple-element.168) | copy-start | bytes 274
  25.9 78.3 %collective-permute-start.4 = (f32[256,2,132]{2,0,1:T(8,128)}, f32[256,2,132]{2,0,1:T(8,128)}, u32[]{:S(2)}, u32[]{:S(2)}) collective-permute-start(f32[256,2,132]{2,0,1:T(8,128)} %pad_maximum_fusion.3), channel_id=1, source_target_pairs={{0,4},{4,8},{8,12},{12,16},{16,20},{20,24},{24,28},{28,32},{32,36}... | collective-permute-start | bytes 811016 | tf_op jit(solution)/shard_map/ppermute | solution.py:32
  32.5 0.7 copy-start.9
  33.4 0.7 copy-start.8
  35.0 2.9 copy-start.2
  35.7 3.2 copy-start.7
  36.5 67.7 %collective-permute-start.5 = (f32[256,2,132]{2,0,1:T(8,128)}, f32[256,2,132]{2,0,1:T(8,128)}, u32[]{:S(2)}, u32[]{:S(2)}) collective-permute-start(f32[256,2,132]{2,0,1:T(8,128)} %pad_maximum_fusion.4), channel_id=1, source_target_pairs={{4,0},{8,4},{12,8},{16,12},{20,16},{24,20},{28,24},{32,28},{36,32}... | collective-permute-start | bytes 811016 | tf_op jit(solution)/shard_map/ppermute | solution.py:32
  45.4 18.6 %collective-permute-start.2 = (bf16[256,6,2]{2,1,0:T(8,128)(2,1)S(1)}, bf16[256,6,2]{2,1,0:T(8,128)(2,1)S(1)}, u32[]{:S(2)}, u32[]{:S(2)}) collective-permute-start(bf16[256,6,2]{2,1,0:T(8,128)(2,1)S(1)} %get-tuple-element.158), channel_id=1, source_target_pairs={{0,1},{1,2},{2,3},{3,0},{4,5},{5,6},{6,7},{7,4},{8,9},{9,10},{10,1... | collective-permute-start | bytes 18440 | tf_op jit(solution)/shard_map/ppermute | solution.py:20
  47.2 19.3 %collective-permute-start.3 = (bf16[256,6,2]{2,1,0:T(8,128)(2,1)S(1)}, bf16[256,6,2]{2,1,0:T(8,128)(2,1)S(1)}, u32[]{:S(2)}, u32[]{:S(2)}) collective-permute-start(bf16[256,6,2]{2,1,0:T(8,128)(2,1)S(1)} %get-tuple-element.157), channel_id=1, source_target_pairs={{1,0},{2,1},{3,2},{0,3},{5,4},{6,5},{7,6},{4,7},{9,8},{10,9},{11,1... | collective-permute-start | bytes 18440 | tf_op jit(solution)/shard_map/ppermute | solution.py:22
  98.8 1.2 copy-start.1
  100.4 1.8 copy-start.5
  104.2 0.9 copy-start.3
  104.2 1.0 copy-start.4
  107.3 6.9 %collective-permute-start.6 = (f32[256,2,2]{2,0,1:T(8,128)}, f32[256,2,2]{2,0,1:T(8,128)S(1)}, u32[]{:S(2)}, u32[]{:S(2)}) collective-permute-start(f32[256,2,2]{2,0,1:T(8,128)} %get-tuple-element.156), channel_id=1, source_target_pairs={{0,3},{1,0},{2,1},{3,2},{4,7},{5,4},{6,5},{7,6},{8,11},{9,8},{10,9... | collective-permute-start | bytes 12296 | tf_op jit(solution)/shard_map/ppermute | solution.py:38
  108.7 6.7 %collective-permute-start.7 = (f32[256,2,2]{2,0,1:T(8,128)S(1)}, f32[256,2,2]{2,0,1:T(8,128)S(1)}, u32[]{:S(2)}, u32[]{:S(2)}) collective-permute-start(f32[256,2,2]{2,0,1:T(8,128)S(1)} %get-tuple-element.155), channel_id=1, source_target_pairs={{0,1},{1,2},{2,3},{3,0},{4,5},{5,6},{6,7},{7,4},{8,9},{9,10},{10,1... | collective-permute-start | bytes 12296 | tf_op jit(solution)/shard_map/ppermute | solution.py:38
Sparse Core Ops, SparseCore 0:
  104.3 265.2 all-reduce.53
where the time goes:
time: 383 us; the launch traced here: 380 us
  waiting for transfers between devices  272 us (71%)
  local copies, waits for them, and re-layouts  51.7 us (13%)
  starting transfers between devices  19 us (5%)
  between operations  14.6 us (4%)
  other arithmetic  14.5 us (4%)
  matrix products  8.76 us (2%)
    psum x1, waiting for transfers between devices, per_device(): grad_sum = lax.psum(local_grad, ('lat', 'lon'))  253 us
    another operation x2, local copies, waits for them, and re-layouts, per_device(): jnp.stack([extended[:, i + j, l:l + lon_cols] for j in range(window) for...  21.3 us
    ppermute x2, waiting for transfers between devices, padded(): lax.ppermute(tail, axis, [(i, (i + 1) % count) for i in range(ends)])  12.9 us
    slice x5, local copies, waits for them, and re-layouts, per_device(): extended[:, i + j, l:l + lon_cols]  11 us
    unnamed x32, local copies, waits for them, and re-layouts  8.27 us
    ppermute x2, starting transfers between devices, padded(): lax.ppermute(tail, axis, [(i, (i + 1) % count) for i in range(ends)])  8.08 us
    ppermute x2, starting transfers between devices, from_behind(): return lax.ppermute(block, axis, route)  7.75 us
  transfers between devices with their start and end apart: 9, of which 4 were waited for; matrix products, arithmetic and copies ran while one was open for 18% of the time, Pallas kernels for 0%

commit v1 on v0

v1 whole, which is shorter than its diff:
```python
import functools
import math

import jax
import jax.numpy as jnp
from jax import lax
from jax.experimental import pallas as pl
from jax.experimental.pallas import tpu as pltpu
from jax.sharding import PartitionSpec as P

BF = jnp.bfloat16
F32 = jnp.float32
MESH = pl.DeviceIdType.MESH
C = 256
K = 9
LANES = 128
NY, NZ, NX = 4, 8, 4
NXY = NX * NY
N_LAT, N_LON = 64, 4
N_ROWS = 128
PIECE = 144
ZROWS = 18
ZPAD = 32
NT = (((1,), (1,)), ((), ()))
TN = (((0,), (0,)), ((), ()))
NN = (((1,), (0,)), ((), ()))


def dot(a, b, dims=NN):
    return lax.dot_general(a, b, dims, preferred_element_type=F32)


def kernel(
    feat, cot, w, table, rng, ids,
    out, ig, wg,
    fx, e_send, e_recv, bmat, bhal, big, bo, bgk, igp, gr, egs, egr,
    cs, cr, own, xs, xr, zf, zs, zr, gz, ga,
    f_ss, f_rs, e_ss, e_rs, g_ss, g_rs, h_ss, h_rs, c_ss, c_rs,
    x_ss, x_rs, z_ss, z_rs, gz_ss, gz_rs, gx_ss, gx_rs, gc_ss, gc_rs,
):
    la, lo = lax.axis_index("lat"), lax.axis_index("lon")
    y, z, xh = la // 16, (la // 2) % 8, la % 2
    xl, core = lo // 2, lo % 2
    x = xh * 2 + xl
    me_n = y * 4 + x
    sibling = (la, lo + 1 - 2 * core)

    def lat_peer(dl):
        return (lax.rem(la + dl + N_LAT, N_LAT), lo)

    def edge_peer(s):
        dl, dc = s // 2 - 1, 2 * (s % 2) - 1
        return (lax.rem(la + dl + N_LAT, N_LAT), lax.rem(lo + dc + N_LON, N_LON))

    def xy_peer(i):
        py, px = (y + i // 4) % 4, (x + i % 4) % 4
        return ((py * 8 + z) * 2 + px // 2, (px % 2) * 2 + core)

    def z_peer(i):
        return ((y * 8 + (z + i) % 8) * 2 + xh, lo)

    barrier = pltpu.get_barrier_semaphore()

    def greet(peer):
        pl.semaphore_signal(barrier, inc=1, device_id=peer, device_id_type=MESH)

    greet(lat_peer(-1))
    greet(lat_peer(1))
    for s in range(6):
        greet(edge_peer(s))
    greet(sibling)

    def greet_xy(i, _):
        greet(xy_peer(i))
        return 0

    def greet_z(i, _):
        greet(z_peer(i))
        return 0

    lax.fori_loop(1, NXY, greet_xy, 0)
    lax.fori_loop(1, NZ, greet_z, 0)

    rho = lax.broadcasted_iota(jnp.int32, (16, 2 * LANES), 0)
    col = lax.broadcasted_iota(jnp.int32, (16, 2 * LANES), 1)
    edge_i = rho % 4
    edge_col = jnp.where(edge_i < 2, edge_i, edge_i + LANES - 4)
    sel = ((rho < 8) & (col == (rho // 4) * LANES + edge_col)).astype(F32).astype(BF)
    e_send[...] = dot(sel, feat[...], NT).astype(BF)

    pl.semaphore_wait(barrier, 2 + 6 + 1 + (NXY - 1) + (NZ - 1))

    def remote(src, dst, ss, rs, peer):
        return pltpu.make_async_remote_copy(
            src_ref=src, dst_ref=dst, send_sem=ss, recv_sem=rs, device_id=peer, device_id_type=MESH
        )

    feat_copies = [
        remote(feat, fx.at[1], f_ss.at[0], f_rs.at[1], lat_peer(-1)),
        remote(feat, fx.at[0], f_ss.at[1], f_rs.at[0], lat_peer(1)),
    ]
    for c in feat_copies:
        c.start()
    edge_copies = [
        remote(e_send, e_recv.at[5 - s], e_ss.at[s], e_rs.at[5 - s], edge_peer(s)) for s in range(6)
    ]
    for c in edge_copies:
        c.start()

    diag = lax.broadcasted_iota(jnp.int32, (LANES, LANES), 0) - lax.broadcasted_iota(
        jnp.int32, (LANES, LANES), 1
    ) + 2
    hr = lax.broadcasted_iota(jnp.int32, (16, LANES), 0)
    hp = lax.broadcasted_iota(jnp.int32, (16, LANES), 1)
    row_ids, row_act = [], []
    for t in range(2):
        g = la * 2 + t
        r0, r1 = rng[0, g], rng[1, g]
        row_ids.append([ids[j, g] for j in range(5)])
        row_act.append(
            [
                (j >= r0) & (j < r1) & (g + j - 2 >= 0) & (g + j - 2 < N_ROWS)
                for j in range(5)
            ]
        )
    zero_block = jnp.zeros((LANES, LANES), BF)

    def build(k, _):
        coef = [
            [
                [jnp.where(row_act[t][j], table[k, l, row_ids[t][j]], 0.0) for l in range(5)]
                for j in range(5)
            ]
            for t in range(2)
        ]
        for t in range(2):
            lanes = slice(t * LANES, (t + 1) * LANES)
            for e in range(6):
                j = e - t
                rows = slice((e % 2) * LANES, (e % 2 + 1) * LANES)
                if j < 0 or j > 4:
                    bmat[k, e // 2, rows, lanes] = zero_block
                    continue
                v = jnp.zeros((LANES, LANES), F32)
                for l in range(5):
                    v = jnp.where(diag == l, coef[t][j][l], v)
                bmat[k, e // 2, rows, lanes] = v.astype(BF)
            for s in range(6):
                v = jnp.zeros((16, LANES), F32)
                for r in range(2):
                    j = (s // 2) * 2 + r - t
                    if j < 0 or j > 4:
                        continue
                    if s % 2 == 0:
                        outer = (hr == r * 4 + 2) & (hp == 0) | (hr == r * 4 + 3) & (hp == 1)
                        inner = (hr == r * 4 + 3) & (hp == 0)
                        v = jnp.where(outer, coef[t][j][0], jnp.where(inner, coef[t][j][1], v))
                    else:
                        outer = (hr == r * 4) & (hp == 126) | (hr == r * 4 + 1) & (hp == 127)
                        inner = (hr == r * 4) & (hp == 127)
                        v = jnp.where(outer, coef[t][j][4], jnp.where(inner, coef[t][j][3], v))
                bhal[k, s * 16 : s * 16 + 16, lanes] = v.astype(BF)
        return 0

    lax.fori_loop(0, K, build, 0)

    def basis_grad(m, _):
        cols = pl.ds(pl.multiple_of(m * 256, 256), 256)
        g = dot(w[:, cols], cot[...], TN)
        big[0, cols, :] = g[:, :LANES]
        big[1, cols, :] = g[:, LANES:]
        return 0

    lax.fori_loop(0, K, basis_grad, 0)
    for k in range(K):
        for t in range(2):
            bgk[k, :, t * LANES : (t + 1) * LANES] = big[t, pl.ds(k, C, stride=K), :].astype(BF)

    def input_grad(dl):
        acc = dot(bgk[0], bmat[0, dl], NT)
        for k in range(1, K):
            acc += dot(bgk[k], bmat[k, dl], NT)
        return acc

    igp[0] = input_grad(0).astype(BF)
    igp[1] = input_grad(2).astype(BF)
    acc = dot(bhal[0], bgk[0], NT)
    for k in range(1, K):
        acc += dot(bhal[k], bgk[k], NT)
    for s in range(6):
        egs[s] = acc[s * 16 : s * 16 + 16].astype(BF)
    grad_copies = [
        remote(igp.at[0], gr.at[1], g_ss.at[0], g_rs.at[1], lat_peer(-1)),
        remote(igp.at[1], gr.at[0], g_ss.at[1], g_rs.at[0], lat_peer(1)),
    ] + [remote(egs.at[s], egr.at[s], h_ss.at[s], h_rs.at[s], edge_peer(s)) for s in range(6)]
    for c in grad_copies:
        c.start()

    for c in feat_copies + edge_copies:
        c.wait()
    halo = e_recv[...].reshape(96, C)
    for k in range(K):
        acc = dot(feat[...], bmat[k, 1]) + dot(fx[0], bmat[k, 0]) + dot(fx[1], bmat[k, 2])
        acc += dot(halo, bhal[k], TN)
        big[0, pl.ds(k, C, stride=K), :] = acc[:, :LANES]
        big[1, pl.ds(k, C, stride=K), :] = acc[:, LANES:]

    def to_tiles(v):
        return jnp.concatenate(
            [v[:, :LANES].reshape(16, 8, LANES), v[:, LANES:].reshape(16, 8, LANES)], axis=1
        )

    theirs = cot[pl.ds(pl.multiple_of(128 * (1 - core), 128), 128), :]
    mine = cot[pl.ds(pl.multiple_of(128 * core, 128), 128), :]
    for m in range(K):
        rows = slice(m * 256, m * 256 + 256)
        bo[rows, :LANES] = big[0, rows, :].astype(BF)
        bo[rows, LANES:] = big[1, rows, :].astype(BF)
        cs[:, m * 16 : m * 16 + 16, :] = to_tiles(dot(theirs, bo[rows, :], NT)).astype(BF)
    core_copy = remote(cs, cr, c_ss, c_rs, sibling)
    core_copy.start()
    for m in range(K):
        rows = slice(m * 256, m * 256 + 256)
        own[:, m * 16 : m * 16 + 16, :] = to_tiles(dot(mine, bo[rows, :], NT))
    core_copy.wait()

    def reduce_core(n, _):
        xs[n] = (own[n] + cr[n].astype(F32)).astype(BF)
        return 0

    lax.fori_loop(0, NXY, reduce_core, 0)

    def xy_index(i):
        return ((y + i // 4) % 4) * 4 + (x + i % 4) % 4

    def xy_copy(i):
        return remote(xs.at[xy_index(i)], xr.at[i], x_ss.at[i], x_rs.at[i], xy_peer(i))

    def xy_start(i, _):
        xy_copy(i).start()
        return 0

    lax.fori_loop(1, NXY, xy_start, 0)

    acc = dot(w[:, :256], bo[:256, :])
    for m in range(1, K):
        acc += dot(w[:, m * 256 : m * 256 + 256], bo[m * 256 : m * 256 + 256, :])
    out[...] = acc.astype(BF)

    def xy_add(i, total):
        xy_copy(i).wait()
        return total + xr[i].astype(F32)

    zf[0:PIECE, :] = lax.fori_loop(1, NXY, xy_add, xs[me_n].astype(F32))
    zf[PIECE:, :] = jnp.zeros((ZPAD - ZROWS + 2, LANES), F32)
    for i in range(NZ):
        zs[i] = zf[ZROWS * i : ZROWS * i + ZPAD, :].astype(BF)

    def z_copy(i):
        return remote(zs.at[(z + i) % 8], zr.at[i], z_ss.at[i], z_rs.at[i], z_peer(i))

    def z_start(i, _):
        z_copy(i).start()
        return 0

    def z_add(i, total):
        z_copy(i).wait()
        return total + zr[i].astype(F32)

    lax.fori_loop(1, NZ, z_start, 0)
    total = lax.fori_loop(1, NZ, z_add, zs[z].astype(F32))
    gz[z] = (total * F32(1.0 / math.sqrt(N_ROWS * N_LON * LANES))).astype(BF)

    def gz_copy(i):
        return remote(gz.at[z], gz.at[z], gz_ss.at[i], gz_rs.at[i], z_peer(i))

    def gz_landed(i):
        src = (z + 8 - i) % 8
        return remote(gz.at[src], gz.at[src], gz_ss.at[i], gz_rs.at[i], z_peer(i))

    def gz_start(i, _):
        gz_copy(i).start()
        return 0

    def gz_wait(i, _):
        gz_copy(i).wait_send()
        gz_landed(i).wait_recv()
        return 0

    lax.fori_loop(1, NZ, gz_start, 0)
    lax.fori_loop(1, NZ, gz_wait, 0)
    for i in range(NZ):
        zf[ZROWS * i : ZROWS * i + ZPAD, :] = gz[i].astype(F32)
    ga[core, me_n] = zf[0:PIECE, :].astype(BF)

    def gx_copy(i):
        return remote(ga.at[core, me_n], ga.at[core, me_n], gx_ss.at[i], gx_rs.at[i], xy_peer(i))

    def from_index(i):
        return ((y + 4 - i // 4) % 4) * 4 + (x + 4 - i % 4) % 4

    def gx_landed(i):
        n = from_index(i)
        return remote(ga.at[core, n], ga.at[core, n], gx_ss.at[i], gx_rs.at[i], xy_peer(i))

    def gc_copy(i):
        n = from_index(i)
        return remote(ga.at[core, n], ga.at[core, n], gc_ss.at[i], gc_rs.at[i], sibling)

    def gc_landed(i):
        n = from_index(i)
        return remote(ga.at[1 - core, n], ga.at[1 - core, n], gc_ss.at[i], gc_rs.at[i], sibling)

    def gx_start(i, _):
        gx_copy(i).start()
        return 0

    def gx_pass(i, _):
        gx_landed(i).wait_recv()
        gc_copy(i).start()
        return 0

    lax.fori_loop(1, NXY, gx_start, 0)
    gc_copy(0).start()

    for c in grad_copies:
        c.wait()
    edges = egr[0].astype(F32)
    for s in range(1, 6):
        edges += egr[s].astype(F32)
    acc = input_grad(1) + gr[0].astype(F32) + gr[1].astype(F32)
    edge_hi = edges.astype(BF)
    edge_lo = (edges - edge_hi.astype(F32)).astype(BF)
    acc += dot(edge_hi, sel, TN) + dot(edge_lo, sel, TN)
    ig[...] = acc.astype(BF)

    lax.fori_loop(1, NXY, gx_pass, 0)

    def gx_drain(i, _):
        gx_copy(i).wait_send()
        return 0

    def gc_drain(i, _):
        gc_copy(i).wait_send()
        gc_landed(i).wait_recv()
        return 0

    lax.fori_loop(0, NXY, gc_drain, 0)
    lax.fori_loop(1, NXY, gx_drain, 0)

    for h in range(2):
        for m in range(K):
            v = ga[h, :, m * 16 : m * 16 + 16, :].astype(F32)
            rows = slice(h * 128, h * 128 + 128)
            wg[rows, m * 256 : m * 256 + LANES] = v[:, :8].reshape(128, LANES)
            wg[rows, m * 256 + LANES : m * 256 + 256] = v[:, 8:].reshape(128, LANES)


def per_device(features, weight, filter_table, row_range, basis_id, cotangent):
    vmem = pl.BlockSpec(memory_space=pltpu.VMEM)
    smem = pl.BlockSpec(memory_space=pltpu.SMEM)
    dma = pltpu.SemaphoreType.DMA
    scratch = [
        pltpu.VMEM((2, C, 256), BF),
        pltpu.VMEM((16, C), BF),
        pltpu.VMEM((6, 16, C), BF),
        pltpu.VMEM((K, 3, 256, 256), BF),
        pltpu.VMEM((K, 96, 256), BF),
        pltpu.VMEM((2, C * K, LANES), F32),
        pltpu.VMEM((C * K, 256), BF),
        pltpu.VMEM((K, C, 256), BF),
        pltpu.VMEM((2, C, 256), BF),
        pltpu.VMEM((2, C, 256), BF),
        pltpu.VMEM((6, 16, C), BF),
        pltpu.VMEM((6, 16, C), BF),
        pltpu.VMEM((NXY, PIECE, LANES), BF),
        pltpu.VMEM((NXY, PIECE, LANES), BF),
        pltpu.VMEM((NXY, PIECE, LANES), F32),
        pltpu.VMEM((NXY, PIECE, LANES), BF),
        pltpu.VMEM((NXY, PIECE, LANES), BF),
        pltpu.VMEM((PIECE + ZPAD - ZROWS + 2, LANES), F32),
        pltpu.VMEM((NZ, ZPAD, LANES), BF),
        pltpu.VMEM((NZ, ZPAD, LANES), BF),
        pltpu.VMEM((NZ, ZPAD, LANES), BF),
        pltpu.VMEM((2, NXY, PIECE, LANES), BF),
        dma((2,)), dma((2,)), dma((6,)), dma((6,)), dma((2,)), dma((2,)), dma((6,)), dma((6,)),
        dma, dma, dma((NXY,)), dma((NXY,)), dma((NZ,)), dma((NZ,)), dma((NZ,)), dma((NZ,)),
        dma((NXY,)), dma((NXY,)), dma((NXY,)), dma((NXY,)),
    ]
    out, ig, wg = pl.pallas_call(
        kernel,
        out_shape=(
            jax.ShapeDtypeStruct((C, 256), BF),
            jax.ShapeDtypeStruct((C, 256), BF),
            jax.ShapeDtypeStruct((C, C * K), F32),
        ),
        in_specs=[vmem, vmem, vmem, smem, smem, smem],
        out_specs=(vmem, vmem, vmem),
        scratch_shapes=scratch,
        compiler_params=pltpu.CompilerParams(
            collective_id=0, has_side_effects=True, vmem_limit_bytes=56 * 1024 * 1024
        ),
    )(
        features.reshape(C, 256),
        cotangent.reshape(C, 256),
        weight,
        filter_table.transpose(1, 2, 0),
        row_range.T,
        basis_id.T,
    )
    return out.reshape(C, 2, LANES), ig.reshape(C, 2, LANES), wg


def solution(mesh):
    in_specs = (P(None, "lat", "lon"), P(), P(), P(), P(), P(None, "lat", "lon"))
    out_specs = (P(None, "lat", "lon"), P(None, "lat", "lon"), P())
    return jax.shard_map(
        per_device, mesh=mesh, in_specs=in_specs, out_specs=out_specs, check_vma=False
    )
```

time: 383 us -> 71.3 us (0.19)
  waiting for transfers between devices: 272 us -> 0 us
  Pallas kernels: 0 us -> 62.3 us
  local copies, waits for them, and re-layouts: 51.7 us -> 8.11 us
  starting transfers between devices: 19 us -> 0 us
  other arithmetic: 14.5 us -> 0 us
  between operations: 14.6 us -> 0.64 us
  matrix products: 8.76 us -> 0 us
    psum x1 -> x0, waiting for transfers between devices: 253 us -> none  [per_device(): grad_sum = lax.psum(local_grad, ('lat', 'lon'))]
    pallas_call x0 -> x1, Pallas kernels: none -> 62.3 us  [per_device(): pl.pallas_call(kernel, out_shape=(jax.ShapeDtypeStruct((C, 256), BF), jax...]
    another operation x5 -> x0, local copies, waits for them, and re-layouts: 23.1 us -> none  [the longest x2 21.3 us: per_device(): jnp.stack([extended[:, i + j, l:l + lon_cols] for j in range(window) for...]
    ppermute x8 -> x0, waiting for transfers between devices: 19.1 us -> none  [the longest x2 12.9 us: padded(): lax.ppermute(tail, axis, [(i, (i + 1) % count) for i in range(ends)])]
    ppermute x8 -> x0, starting transfers between devices: 18.9 us -> none  [the longest x2 8.08 us: padded(): lax.ppermute(tail, axis, [(i, (i + 1) % count) for i in range(ends)])]
    slice x14 -> x0, local copies, waits for them, and re-layouts: 14.9 us -> none  [the longest x5 11 us: per_device(): extended[:, i + j, l:l + lon_cols]]
    dot_general x16 -> x0, matrix products: 8.76 us -> none  [the longest x10 2.77 us: per_device(): jnp.einsum('ckp,kl->clp', basis_grad[:, :, i], filter_coef[i, :, j, :], p...]
    another operation x9 -> x0, other arithmetic: 6.59 us -> none  [the longest x8 6.18 us: per_device(): ext_sum = jnp.stack(ext_list, axis=1)]
  transfers between devices with their start and end apart: 9 -> 0, of which waited for: 4 -> 0; matrix products, arithmetic and copies ran while one was open for 18% -> 0% of each run, Pallas kernels for 0% -> 0%
where the time goes in v1:
time: 71.3 us; the launch traced here: 71.1 us
  Pallas kernels  62.3 us (87%)
  local copies, waits for them, and re-layouts  8.11 us (11%)
    pallas_call x1, Pallas kernels, per_device(): pl.pallas_call(kernel, out_shape=(jax.ShapeDtypeStruct((C, 256), BF), jax...  62.3 us
    unnamed x1, local copies, waits for them, and re-layouts  3.22 us
    reshape x2, local copies, waits for them, and re-layouts, per_device(): return (out.reshape(C, 2, LANES), ig.reshape(C, 2, LANES), wg)  3.19 us
    reshape x1, local copies, waits for them, and re-layouts, per_device(): cotangent.reshape(C, 256)  1.7 us

profile of v1, /device:TPU:1, one launch (start us, length us, event | category | flops | bytes accessed | tf_op | source)
XLA Modules:
  0.0 71.1 jit_solution(2051885893934138272)
XLA Ops:
  0.6 1.7 %copy_bitcast_fusion = (bf16[256,256]{1,0:T(8,128)(2,1)}, bf16[256,256]{1,0:T(8,128)(2,1)}) fusion(bf16[32,8,2,128]{3,2,1,0:T(2,128)(2,1)} %bitcast.9, bf16[32,8,2,128]{3,2,1,0:T(2,128)(2,1)} %bitcast.10), kind=kLoop, calls=%fused_computation | loop fusion | bytes 524288 | tf_op jit(solution)/shard_map/reshape | solution.py:405
  2.3 62.3 %shard_map.85 = (bf16[256,256]{1,0:T(8,128)(2,1)}, bf16[256,256]{1,0:T(8,128)(2,1)}, f32[256,2304]{1,0:T(8,128)}) custom-call(bf16[256,256]{1,0:T(8,128)(2,1)} %get-tuple-element.10.feat, bf16[256,256]{1,0:T(8,128)(2,1)} %get-tuple-element.9.cot, bf16[256,2304]{1,0:T(8,128)(2,1)} %w.1, f32[9,5,16]{2,1,0:T(8,128)} %bitcast.11, s32[2,128]{1,0:T(2,128)} %bitcast.13, ...), custom_call_target="tpu_custom_call" | custom-call | tf_op jit(solution)/shard_map/pallas_call | solution.py:390
  64.6 1.6 %reshape.20 = bf16[256,2,128]{2,1,0:T(2,128)(2,1)} reshape(bf16[256,256]{1,0:T(8,128)(2,1)} %get-tuple-element.6) | data formatting | bytes 262144 | tf_op jit(solution)/shard_map/reshape | solution.py:411
  66.2 1.6 %reshape.21 = bf16[256,2,128]{2,1,0:T(2,128)(2,1)} reshape(bf16[256,256]{1,0:T(8,128)(2,1)} %get-tuple-element.7) | data formatting | bytes 262144 | tf_op jit(solution)/shard_map/reshape | solution.py:411
  67.8 3.2 %copy.14 = f32[256,2304]{1,0:T(8,128)} copy(f32[256,2304]{1,0:T(8,128)} %get-tuple-element.16) | data formatting | bytes 4718592

commit v2 on v1

v2 whole, which is shorter than its diff:
```python
import functools
import math

import jax
import jax.numpy as jnp
from jax import lax
from jax.experimental import pallas as pl
from jax.experimental.pallas import tpu as pltpu
from jax.sharding import PartitionSpec as P

BF = jnp.bfloat16
F32 = jnp.float32
MESH = pl.DeviceIdType.MESH
C = 256
K = 9
LANES = 128
NZ = 8
N_LAT, N_LON = 64, 4
N_ROWS = 128
HALF = C * K // 2
TILES = HALF // LANES
NT = (((1,), (1,)), ((), ()))
TN = (((0,), (0,)), ((), ()))
NN = (((1,), (0,)), ((), ()))


def dot(a, b, dims=NN):
    return lax.dot_general(a, b, dims, preferred_element_type=F32)


def kernel(
    feat, cot, w_hbm, table, rng, ids,
    out, ig, wg,
    w, fx, e_send, e_recv, bmat, bhal, big, bo, bgk, igp, gr, egs, egr,
    cs, cr, own, s1, r1, zf, s2, r2, zg, s3, r3, g1, g2,
    w_sem, f_ss, f_rs, e_ss, e_rs, g_ss, g_rs, h_ss, h_rs, c_ss, c_rs,
    s1_ss, s1_rs, s2_ss, s2_rs, s3_ss, s3_rs,
    g1_ss, g1_rs, g2_ss, g2_rs, g3_ss, g3_rs, gc_ss, gc_rs,
):
    la, lo = lax.axis_index("lat"), lax.axis_index("lon")
    y, z, xh = la // 16, (la // 2) % 8, la % 2
    xl, core = lo // 2, lo % 2
    x = xh * 2 + xl
    sibling = (la, lo + 1 - 2 * core)
    me1, me2 = (y, x), (x, y)

    def lat_peer(dl):
        return (lax.rem(la + dl + N_LAT, N_LAT), lo)

    def edge_peer(s):
        dl, dc = s // 2 - 1, 2 * (s % 2) - 1
        return (lax.rem(la + dl + N_LAT, N_LAT), lax.rem(lo + dc + N_LON, N_LON))

    def y_peer(i):
        return ((((y + i) % 4) * 8 + z) * 2 + xh, lo)

    def x_peer(i):
        px = (x + i) % 4
        return ((y * 8 + z) * 2 + px // 2, (px % 2) * 2 + core)

    def z_peer(i):
        return ((y * 8 + (z + i) % 8) * 2 + xh, lo)

    peer1, peer2 = (y_peer, x_peer), (x_peer, y_peer)

    barrier = pltpu.get_barrier_semaphore()
    peers = [lat_peer(-1), lat_peer(1)] + [edge_peer(s) for s in range(6)]
    peers += [y_peer(i) for i in (1, 2, 3)] + [x_peer(i) for i in (1, 3)]
    peers += [z_peer(i) for i in range(1, NZ)]
    for peer in peers:
        pl.semaphore_signal(barrier, inc=1, device_id=peer, device_id_type=MESH)
    w_copy = pltpu.make_async_copy(w_hbm, w, w_sem)
    w_copy.start()

    rho = lax.broadcasted_iota(jnp.int32, (16, 2 * LANES), 0)
    col = lax.broadcasted_iota(jnp.int32, (16, 2 * LANES), 1)
    edge_i = rho % 4
    edge_col = jnp.where(edge_i < 2, edge_i, edge_i + LANES - 4)
    sel = ((rho < 8) & (col == (rho // 4) * LANES + edge_col)).astype(F32).astype(BF)
    e_send[...] = dot(sel, feat[...], NT).astype(BF)

    pl.semaphore_wait(barrier, len(peers))

    def remote(src, dst, ss, rs, peer):
        return pltpu.make_async_remote_copy(
            src_ref=src, dst_ref=dst, send_sem=ss, recv_sem=rs, device_id=peer, device_id_type=MESH
        )

    half_rows = [slice(0, 128), slice(128, 256)]
    feat_copies = [
        [
            remote(
                feat.at[half_rows[h]], fx.at[1, half_rows[h]], f_ss.at[h, 0], f_rs.at[h, 1], lat_peer(-1)
            ),
            remote(
                feat.at[half_rows[h]], fx.at[0, half_rows[h]], f_ss.at[h, 1], f_rs.at[h, 0], lat_peer(1)
            ),
        ]
        for h in range(2)
    ]
    edge_copies = [
        remote(e_send, e_recv.at[5 - s], e_ss.at[s], e_rs.at[5 - s], edge_peer(s)) for s in range(6)
    ]
    for c in feat_copies[0] + edge_copies + feat_copies[1]:
        c.start()

    diag = lax.broadcasted_iota(jnp.int32, (LANES, LANES), 0) - lax.broadcasted_iota(
        jnp.int32, (LANES, LANES), 1
    ) + 2
    hr = lax.broadcasted_iota(jnp.int32, (16, LANES), 0)
    hp = lax.broadcasted_iota(jnp.int32, (16, LANES), 1)
    row_ids, row_act = [], []
    for t in range(2):
        g = la * 2 + t
        r0, r1_ = rng[0, g], rng[1, g]
        row_ids.append([ids[j, g] for j in range(5)])
        row_act.append(
            [
                (j >= r0) & (j < r1_) & (g + j - 2 >= 0) & (g + j - 2 < N_ROWS)
                for j in range(5)
            ]
        )
    zero_block = jnp.zeros((LANES, LANES), BF)

    def build(k, _):
        coef = [
            [
                [jnp.where(row_act[t][j], table[k, l, row_ids[t][j]], 0.0) for l in range(5)]
                for j in range(5)
            ]
            for t in range(2)
        ]
        for t in range(2):
            lanes = slice(t * LANES, (t + 1) * LANES)
            for e in range(6):
                j = e - t
                rows = slice((e % 2) * LANES, (e % 2 + 1) * LANES)
                if j < 0 or j > 4:
                    bmat[k, e // 2, rows, lanes] = zero_block
                    continue
                v = jnp.zeros((LANES, LANES), F32)
                for l in range(5):
                    v = jnp.where(diag == l, coef[t][j][l], v)
                bmat[k, e // 2, rows, lanes] = v.astype(BF)
            for s in range(6):
                v = jnp.zeros((16, LANES), F32)
                for r in range(2):
                    j = (s // 2) * 2 + r - t
                    if j < 0 or j > 4:
                        continue
                    if s % 2 == 0:
                        outer = (hr == r * 4 + 2) & (hp == 0) | (hr == r * 4 + 3) & (hp == 1)
                        inner = (hr == r * 4 + 3) & (hp == 0)
                        v = jnp.where(outer, coef[t][j][0], jnp.where(inner, coef[t][j][1], v))
                    else:
                        outer = (hr == r * 4) & (hp == 126) | (hr == r * 4 + 1) & (hp == 127)
                        inner = (hr == r * 4) & (hp == 127)
                        v = jnp.where(outer, coef[t][j][4], jnp.where(inner, coef[t][j][3], v))
                bhal[k, s * 16 : s * 16 + 16, lanes] = v.astype(BF)
        return 0

    lax.fori_loop(0, K, build, 0)
    for h in range(2):
        zf[h, :, 72:80, :] = jnp.zeros((4, 8, LANES), F32)

    theirs = pl.ds(pl.multiple_of(128 * (1 - core), 128), 128)
    mine = pl.ds(pl.multiple_of(128 * core, 128), 128)
    chunks = [(0, 256), (256, 512), (512, 768), (768, 1024), (1024, 1152)]

    def core_copy(h):
        return remote(cs.at[h], cr.at[h], c_ss.at[h], c_rs.at[h], sibling)

    def basis(h):
        hc = half_rows[h]
        halo = e_recv[:, :, hc].reshape(96, 128)
        for k in range(K):
            acc = dot(feat[hc, :], bmat[k, 1]) + dot(fx[0, hc, :], bmat[k, 0])
            acc += dot(fx[1, hc, :], bmat[k, 2]) + dot(halo, bhal[k], TN)
            rows = pl.ds(h * HALF + k, 128, stride=K)
            big[0, rows, :] = acc[:, :LANES]
            big[1, rows, :] = acc[:, LANES:]
        for a, b in chunks:
            rows = slice(h * HALF + a, h * HALF + b)
            bo[rows, :LANES] = big[0, rows, :].astype(BF)
            bo[rows, LANES:] = big[1, rows, :].astype(BF)
            cs[h, :, a:b] = dot(cot[theirs, :], bo[rows, :], NT).astype(BF)
        core_copy(h).start()

    def weight_rows(h):
        for a, b in chunks:
            own[h, :, a:b] = dot(cot[mine, :], bo[h * HALF + a : h * HALF + b, :], NT)

    def s1_copy(h, i):
        rows = pl.ds(pl.multiple_of(32 * ((me1[h] + i) % 4), 32), 32)
        return remote(s1.at[h, rows], r1.at[h, i], s1_ss.at[h, i], s1_rs.at[h, i], peer1[h](i))

    def s2_copy(h, i):
        n = (me2[h] + i) % 4
        return remote(s2.at[h, n], r2.at[h, i], s2_ss.at[h, i], s2_rs.at[h, i], peer2[h](i))

    def s3_copy(h, i):
        n = (z + i) % 8
        return remote(s3.at[h, n], r3.at[h, i], s3_ss.at[h, i], s3_rs.at[h, i], z_peer(i))

    def g1_copy(h, i, n):
        return remote(g1.at[h, n], g1.at[h, n], g1_ss.at[h, i], g1_rs.at[h, i], z_peer(i))

    def g2_copy(h, i, n):
        return remote(g2.at[h, n], g2.at[h, n], g2_ss.at[h, i], g2_rs.at[h, i], peer2[h](i))

    def piece(h, c, n):
        rows = pl.ds(pl.multiple_of(128 * c + 32 * n, 32), 32)
        return wg.at[rows, h * HALF : (h + 1) * HALF]

    def g3_copy(h, i, n):
        ref = piece(h, core, n)
        return remote(ref, ref, g3_ss.at[h, i], g3_rs.at[h, i], peer1[h](i))

    def gc_copy(h, i, c, n):
        ref = piece(h, c, n)
        return remote(ref, ref, gc_ss.at[h, i], gc_rs.at[h, i], sibling)

    def core_sum(h):
        core_copy(h).wait()
        s1[h] = (own[h] + cr[h].astype(F32)).astype(BF)
        for i in (1, 2, 3):
            s1_copy(h, i).start()

    def sum1(h):
        rows = pl.ds(pl.multiple_of(32 * me1[h], 32), 32)
        total = s1[h, rows, :].astype(F32)
        for i in (1, 2, 3):
            s1_copy(h, i).wait()
            total += r1[h, i].astype(F32)
        for m in range(TILES):
            tile = total[:, m * LANES : (m + 1) * LANES]
            zf[h, :, 8 * m : 8 * m + 8, :] = tile.reshape(4, 8, LANES)
        s2[h] = zf[h].astype(BF)
        for i in (1, 2, 3):
            s2_copy(h, i).start()

    def sum2(h):
        total = s2[h, me2[h]].astype(F32)
        for i in (1, 2, 3):
            s2_copy(h, i).wait()
            total += r2[h, i].astype(F32)
        zg[h] = total
        for i in range(NZ):
            s3[h, i] = zg[h, 9 * i : 9 * i + 16, :].astype(BF)
        for i in range(1, NZ):
            s3_copy(h, i).start()

    def sum3(h):
        total = s3[h, z].astype(F32)
        for i in range(1, NZ):
            s3_copy(h, i).wait()
            total += r3[h, i].astype(F32)
        g1[h, z] = (total * F32(1.0 / math.sqrt(N_ROWS * N_LON * LANES))).astype(BF)
        for i in range(1, NZ):
            g1_copy(h, i, z).start()

    def gather1(h):
        for i in range(1, NZ):
            g1_copy(h, i, z).wait_send()
            g1_copy(h, i, (z + 8 - i) % 8).wait_recv()
        for i in range(NZ):
            zg[h, 9 * i : 9 * i + 16, :] = g1[h, i].astype(F32)
        g2[h, me2[h]] = zg[h].astype(BF)
        for i in (1, 2, 3):
            g2_copy(h, i, me2[h]).start()

    def gather2(h):
        for i in (1, 2, 3):
            g2_copy(h, i, me2[h]).wait_send()
            g2_copy(h, i, (me2[h] + 4 - i) % 4).wait_recv()
        zf[h] = g2[h].astype(F32)
        rows = pl.ds(pl.multiple_of(128 * core + 32 * me1[h], 32), 32)
        for m in range(TILES):
            a = h * HALF + m * LANES
            wg[rows, a : a + LANES] = zf[h, :, 8 * m : 8 * m + 8, :].reshape(32, LANES).astype(BF)
        for i in (1, 2, 3):
            g3_copy(h, i, me1[h]).start()
        gc_copy(h, 0, core, me1[h]).start()

    def gather3(h, i):
        n = (me1[h] + 4 - i) % 4
        g3_copy(h, i, n).wait_recv()
        gc_copy(h, i, core, n).start()

    for c in feat_copies[0] + edge_copies:
        c.wait()
    basis(0)
    weight_rows(0)
    for c in feat_copies[1]:
        c.wait()
    basis(1)
    core_sum(0)
    weight_rows(1)
    core_sum(1)

    w_copy.wait()
    acc = dot(w[:, :256], bo[:256, :])
    for m in range(1, K):
        acc += dot(w[:, m * 256 : m * 256 + 256], bo[m * 256 : m * 256 + 256, :])
    out[...] = acc.astype(BF)

    def basis_grad(m, _):
        cols = pl.ds(pl.multiple_of(m * 256, 256), 256)
        g = dot(w[:, cols], cot[...], TN)
        big[0, cols, :] = g[:, :LANES]
        big[1, cols, :] = g[:, LANES:]
        return 0

    lax.fori_loop(0, K, basis_grad, 0)
    sum1(0)
    sum1(1)
    for k in range(K):
        for t in range(2):
            bgk[k, :, t * LANES : (t + 1) * LANES] = big[t, pl.ds(k, C, stride=K), :].astype(BF)
    sum2(0)
    sum2(1)

    def input_grad(dl):
        acc = dot(bgk[0], bmat[0, dl], NT)
        for k in range(1, K):
            acc += dot(bgk[k], bmat[k, dl], NT)
        return acc

    igp[0] = input_grad(0).astype(BF)
    igp[1] = input_grad(2).astype(BF)
    acc = dot(bhal[0], bgk[0], NT)
    for k in range(1, K):
        acc += dot(bhal[k], bgk[k], NT)
    for s in range(6):
        egs[s] = acc[s * 16 : s * 16 + 16].astype(BF)
    grad_copies = [
        remote(igp.at[0], gr.at[1], g_ss.at[0], g_rs.at[1], lat_peer(-1)),
        remote(igp.at[1], gr.at[0], g_ss.at[1], g_rs.at[0], lat_peer(1)),
    ] + [remote(egs.at[s], egr.at[s], h_ss.at[s], h_rs.at[s], edge_peer(s)) for s in range(6)]
    for c in grad_copies:
        c.start()
    sum3(0)
    sum3(1)
    gather1(0)
    gather1(1)
    gather2(0)
    gather2(1)

    for c in grad_copies:
        c.wait()
    edges = egr[0].astype(F32)
    for s in range(1, 6):
        edges += egr[s].astype(F32)
    acc = input_grad(1) + gr[0].astype(F32) + gr[1].astype(F32)
    edge_hi = edges.astype(BF)
    edge_lo = (edges - edge_hi.astype(F32)).astype(BF)
    acc += dot(edge_hi, sel, TN) + dot(edge_lo, sel, TN)
    ig[...] = acc.astype(BF)

    for i in (1, 3, 2):
        for h in range(2):
            gather3(h, i)
    for h in range(2):
        for i in range(4):
            gc_copy(h, i, core, (me1[h] + 4 - i) % 4).wait_send()
            gc_copy(h, i, 1 - core, (me1[h] + 4 - i) % 4).wait_recv()
        for i in (1, 2, 3):
            g3_copy(h, i, me1[h]).wait_send()


def per_device(features, weight, filter_table, row_range, basis_id, cotangent):
    vmem = pl.BlockSpec(memory_space=pltpu.VMEM)
    smem = pl.BlockSpec(memory_space=pltpu.SMEM)
    hbm = pl.BlockSpec(memory_space=pl.ANY)
    dma = pltpu.SemaphoreType.DMA
    scratch = [
        pltpu.VMEM((C, C * K), BF),
        pltpu.VMEM((2, C, 256), BF),
        pltpu.VMEM((16, C), BF),
        pltpu.VMEM((6, 16, C), BF),
        pltpu.VMEM((K, 3, 256, 256), BF),
        pltpu.VMEM((K, 96, 256), BF),
        pltpu.VMEM((2, C * K, LANES), F32),
        pltpu.VMEM((C * K, 256), BF),
        pltpu.VMEM((K, C, 256), BF),
        pltpu.VMEM((2, C, 256), BF),
        pltpu.VMEM((2, C, 256), BF),
        pltpu.VMEM((6, 16, C), BF),
        pltpu.VMEM((6, 16, C), BF),
        pltpu.VMEM((2, 128, HALF), BF),
        pltpu.VMEM((2, 128, HALF), BF),
        pltpu.VMEM((2, 128, HALF), F32),
        pltpu.VMEM((2, 128, HALF), BF),
        pltpu.VMEM((2, 4, 32, HALF), BF),
        pltpu.VMEM((2, 4, 80, LANES), F32),
        pltpu.VMEM((2, 4, 80, LANES), BF),
        pltpu.VMEM((2, 4, 80, LANES), BF),
        pltpu.VMEM((2, 80, LANES), F32),
        pltpu.VMEM((2, NZ, 16, LANES), BF),
        pltpu.VMEM((2, NZ, 16, LANES), BF),
        pltpu.VMEM((2, NZ, 16, LANES), BF),
        pltpu.VMEM((2, 4, 80, LANES), BF),
        dma,
        dma((2, 2)), dma((2, 2)), dma((6,)), dma((6,)), dma((2,)), dma((2,)), dma((6,)), dma((6,)),
        dma((2,)), dma((2,)),
        dma((2, 4)), dma((2, 4)), dma((2, 4)), dma((2, 4)), dma((2, NZ)), dma((2, NZ)),
        dma((2, NZ)), dma((2, NZ)), dma((2, 4)), dma((2, 4)), dma((2, 4)), dma((2, 4)),
        dma((2, 4)), dma((2, 4)),
    ]
    out, ig, wg = pl.pallas_call(
        kernel,
        out_shape=(
            jax.ShapeDtypeStruct((C, 256), BF),
            jax.ShapeDtypeStruct((C, 256), BF),
            jax.ShapeDtypeStruct((C, C * K), BF),
        ),
        in_specs=[vmem, vmem, hbm, smem, smem, smem],
        out_specs=(vmem, vmem, vmem),
        scratch_shapes=scratch,
        compiler_params=pltpu.CompilerParams(
            collective_id=0, has_side_effects=True, vmem_limit_bytes=48 * 1024 * 1024
        ),
    )(
        features.reshape(C, 256),
        cotangent.reshape(C, 256),
        weight,
        filter_table.transpose(1, 2, 0),
        row_range.T,
        basis_id.T,
    )
    return out.reshape(C, 2, LANES), ig.reshape(C, 2, LANES), wg.astype(F32)


def solution(mesh):
    in_specs = (P(None, "lat", "lon"), P(), P(), P(), P(), P(None, "lat", "lon"))
    out_specs = (P(None, "lat", "lon"), P(None, "lat", "lon"), P())
    return jax.shard_map(
        per_device, mesh=mesh, in_specs=in_specs, out_specs=out_specs, check_vma=False
    )
```

time: 71.3 us -> 63 us (0.88)
  Pallas kernels: 62.3 us -> 54.7 us
  local copies, waits for them, and re-layouts: 8.11 us -> 5.78 us
  other arithmetic: 0 us -> 1.56 us
    pallas_call x1, Pallas kernels: 62.3 us -> 54.7 us  [per_device(): pl.pallas_call(kernel, out_shape=(jax.ShapeDtypeStruct((C, 256), BF), jax...]
    reshape x2, local copies, waits for them, and re-layouts: 3.19 us -> 1.38 us  [per_device(): return (out.reshape(C, 2, LANES), ig.reshape(C, 2, LANES), wg.astype(F32))]
    convert_element_type x0 -> x1, other arithmetic: none -> 1.56 us  [per_device(): return (out.reshape(C, 2, LANES), ig.reshape(C, 2, LANES), wg.astype(F32))]
    unnamed x1 -> x8, local copies, waits for them, and re-layouts: 3.22 us -> 3.4 us
where the time goes in v2:
time: 63 us; the launch traced here: 62.7 us
  Pallas kernels  54.7 us (87%)
  local copies, waits for them, and re-layouts  5.78 us (9%)
  other arithmetic  1.56 us (2%)
  between operations  0.65 us (1%)
    pallas_call x1, Pallas kernels, per_device(): pl.pallas_call(kernel, out_shape=(jax.ShapeDtypeStruct((C, 256), BF), jax...  54.7 us
    unnamed x8, local copies, waits for them, and re-layouts  3.4 us
    convert_element_type x1, other arithmetic, per_device(): return (out.reshape(C, 2, LANES), ig.reshape(C, 2, LANES), wg.astype(F32))  1.56 us
    reshape x2, local copies, waits for them, and re-layouts, per_device(): return (out.reshape(C, 2, LANES), ig.reshape(C, 2, LANES), wg.astype(F32))  1.38 us

profile of v2, /device:TPU:1, one launch (start us, length us, event | category | flops | bytes accessed | tf_op | source)
XLA Modules:
  0.0 62.7 jit_solution(9103376930748245444)
XLA Ops:
  0.6 1.0 %copy_bitcast_fusion = (bf16[256,256]{1,0:T(8,128)(2,1)S(1)}, bf16[256,256]{1,0:T(8,128)(2,1)S(1)}) fusion(bf16[32,8,2,128]{3,2,1,0:T(2,128)(2,1)} %bitcast.12, bf16[32,8,2,128]{3,2,1,0:T(2,128)(2,1)} %bitcast.13), kind=kLoop, calls=%fused_computation | loop fusion | bytes 524288 | tf_op jit(solution)/shard_map/reshape | solution.py:425
  1.6 0.0 copy-start
  1.6 1.3 %copy-done = bf16[256,2304]{1,0:T(8,128)(2,1)S(1)} copy-done((bf16[256,2304]{1,0:T(8,128)(2,1)S(1)}, bf16[256,2304]{1,0:T(8,128)(2,1)}, u32[]{:S(2)}) %copy-start) | copy-done | bytes 1179672
  2.9 0.0 copy-start.1
  2.9 0.8 %copy-done.1 = f32[16,9,5]{0,2,1:T(8,128)S(1)} copy-done((f32[16,9,5]{0,2,1:T(8,128)S(1)}, f32[16,9,5]{0,2,1:T(8,128)}, u32[]{:S(2)}) %copy-start.1) | copy-done | bytes 2904
  3.7 0.0 copy-start.2
  3.7 0.7 %copy-done.2 = s32[128,5]{0,1:T(8,128)S(1)} copy-done((s32[128,5]{0,1:T(8,128)S(1)}, s32[128,5]{0,1:T(8,128)}, u32[]{:S(2)}) %copy-start.2) | copy-done | bytes 2584
  4.4 0.0 copy-start.3
  4.4 0.7 %copy-done.3 = s32[128,2]{0,1:T(2,128)S(1)} copy-done((s32[128,2]{0,1:T(2,128)S(1)}, s32[128,2]{0,1:T(2,128)}, u32[]{:S(2)}) %copy-start.3) | copy-done | bytes 1048
  5.0 54.7 %shard_map.85 = (bf16[256,256]{1,0:T(8,128)(2,1)S(1)}, bf16[256,256]{1,0:T(8,128)(2,1)S(1)}, bf16[256,2304]{1,0:T(8,128)(2,1)S(1)}) custom-call(bf16[256,256]{1,0:T(8,128)(2,1)S(1)} %get-tuple-element.10.feat, bf16[256,256]{1,0:T(8,128)(2,1)S(1)} %get-tuple-element.9.cot, bf16[256,2304]{1,0:T(8,128)(2,1)S(1)} %copy-done, f32[9,5,16]{2,1,0:T(8,128)S(1)} %bitcast.9, ...), custom_call_target="tpu_custom_call" | custom-call | tf_op jit(solution)/shard_map/pallas_call | solution.py:410
  59.8 0.7 %reshape.20 = bf16[256,2,128]{2,1,0:T(2,128)(2,1)} reshape(bf16[256,256]{1,0:T(8,128)(2,1)S(1)} %get-tuple-element.6) | data formatting | bytes 262144 | tf_op jit(solution)/shard_map/reshape | solution.py:431
  60.5 0.7 %reshape.21 = bf16[256,2,128]{2,1,0:T(2,128)(2,1)} reshape(bf16[256,256]{1,0:T(8,128)(2,1)S(1)} %get-tuple-element.7) | data formatting | bytes 262144 | tf_op jit(solution)/shard_map/reshape | solution.py:431
  61.2 1.6 %convert_element_type.3 = f32[256,2304]{1,0:T(8,128)} convert(bf16[256,2304]{1,0:T(8,128)(2,1)S(1)} %get-tuple-element.8) | non-fusion elementwise | flops 589824 | bytes 3538944 | tf_op jit(solution)/shard_map/convert_element_type | solution.py:431
Async XLA Ops:
  1.6 1.3 %copy-start = (bf16[256,2304]{1,0:T(8,128)(2,1)S(1)}, bf16[256,2304]{1,0:T(8,128)(2,1)}, u32[]{:S(2)}) copy-start(bf16[256,2304]{1,0:T(8,128)(2,1)} %w_hbm.1) | copy-start | bytes 3538948
  2.9 0.8 %copy-start.1 = (f32[16,9,5]{0,2,1:T(8,128)S(1)}, f32[16,9,5]{0,2,1:T(8,128)}, u32[]{:S(2)}) copy-start(f32[16,9,5]{0,2,1:T(8,128)} %param.8) | copy-start | bytes 8644
  3.7 0.7 %copy-start.2 = (s32[128,5]{0,1:T(8,128)S(1)}, s32[128,5]{0,1:T(8,128)}, u32[]{:S(2)}) copy-start(s32[128,5]{0,1:T(8,128)} %param.10) | copy-start | bytes 7684
  4.4 0.7 %copy-start.3 = (s32[128,2]{0,1:T(2,128)S(1)}, s32[128,2]{0,1:T(2,128)}, u32[]{:S(2)}) copy-start(s32[128,2]{0,1:T(2,128)} %param.9) | copy-start | bytes 3076

commit v3 on v2

--- a/solution.py
+++ b/solution.py
@@ -29,11 +29,11 @@
 
 
 def kernel(
-    feat, cot, w_hbm, table, rng, ids,
+    feat_hbm, cot_hbm, w_hbm, table_hbm, rng_hbm, ids_hbm,
     out, ig, wg,
-    w, fx, e_send, e_recv, bmat, bhal, big, bo, bgk, igp, gr, egs, egr,
+    raw, feat, cot, table, rng, ids, w, fx, e_send, e_recv, bmat, bhal, big, bo, bgk, igp, gr, egs, egr,
     cs, cr, own, s1, r1, zf, s2, r2, zg, s3, r3, g1, g2,
-    w_sem, f_ss, f_rs, e_ss, e_rs, g_ss, g_rs, h_ss, h_rs, c_ss, c_rs,
+    in_sem, f_ss, f_rs, e_ss, e_rs, g_ss, g_rs, h_ss, h_rs, c_ss, c_rs,
     s1_ss, s1_rs, s2_ss, s2_rs, s3_ss, s3_rs,
     g1_ss, g1_rs, g2_ss, g2_rs, g3_ss, g3_rs, gc_ss, gc_rs,
 ):
@@ -63,14 +63,39 @@
 
     peer1, peer2 = (y_peer, x_peer), (x_peer, y_peer)
 
+    in_copies = [
+        pltpu.make_async_copy(src, dst, in_sem.at[i])
+        for i, (src, dst) in enumerate(
+            [
+                (feat_hbm, raw.at[0]),
+                (table_hbm, table),
+                (rng_hbm, rng),
+                (ids_hbm, ids),
+                (cot_hbm, raw.at[1]),
+                (w_hbm, w),
+            ]
+        )
+    ]
+    for c in in_copies:
+        c.start()
+
     barrier = pltpu.get_barrier_semaphore()
     peers = [lat_peer(-1), lat_peer(1)] + [edge_peer(s) for s in range(6)]
     peers += [y_peer(i) for i in (1, 2, 3)] + [x_peer(i) for i in (1, 3)]
     peers += [z_peer(i) for i in range(1, NZ)]
     for peer in peers:
         pl.semaphore_signal(barrier, inc=1, device_id=peer, device_id_type=MESH)
-    w_copy = pltpu.make_async_copy(w_hbm, w, w_sem)
-    w_copy.start()
+
+    def rows_to_lanes(ref, dst):
+        v = ref[...].astype(F32)
+        dst[:, :LANES] = v[:, 0, :].astype(BF)
+        dst[:, LANES:] = v[:, 1, :].astype(BF)
+
+    def lanes_to_rows(v):
+        return jnp.stack([v[:, :LANES], v[:, LANES:]], axis=1).astype(BF)
+
+    in_copies[0].wait()
+    rows_to_lanes(raw.at[0], feat)
 
     rho = lax.broadcasted_iota(jnp.int32, (16, 2 * LANES), 0)
     col = lax.broadcasted_iota(jnp.int32, (16, 2 * LANES), 1)
@@ -104,6 +129,8 @@
     for c in feat_copies[0] + edge_copies + feat_copies[1]:
         c.start()
 
+    for c in in_copies[1:4]:
+        c.wait()
     diag = lax.broadcasted_iota(jnp.int32, (LANES, LANES), 0) - lax.broadcasted_iota(
         jnp.int32, (LANES, LANES), 1
     ) + 2
@@ -163,6 +190,9 @@
     for h in range(2):
         zf[h, :, 72:80, :] = jnp.zeros((4, 8, LANES), F32)
 
+    in_copies[4].wait()
+    rows_to_lanes(raw.at[1], cot)
+
     theirs = pl.ds(pl.multiple_of(128 * (1 - core), 128), 128)
     mine = pl.ds(pl.multiple_of(128 * core, 128), 128)
     chunks = [(0, 256), (256, 512), (512, 768), (768, 1024), (1024, 1152)]
@@ -298,11 +328,11 @@
     weight_rows(1)
     core_sum(1)
 
-    w_copy.wait()
+    in_copies[5].wait()
     acc = dot(w[:, :256], bo[:256, :])
     for m in range(1, K):
         acc += dot(w[:, m * 256 : m * 256 + 256], bo[m * 256 : m * 256 + 256, :])
-    out[...] = acc.astype(BF)
+    out[...] = lanes_to_rows(acc)
 
     def basis_grad(m, _):
         cols = pl.ds(pl.multiple_of(m * 256, 256), 256)
@@ -355,7 +385,7 @@
     edge_hi = edges.astype(BF)
     edge_lo = (edges - edge_hi.astype(F32)).astype(BF)
     acc += dot(edge_hi, sel, TN) + dot(edge_lo, sel, TN)
-    ig[...] = acc.astype(BF)
+    ig[...] = lanes_to_rows(acc)
 
     for i in (1, 3, 2):
         for h in range(2):
@@ -370,10 +400,15 @@
 
 def per_device(features, weight, filter_table, row_range, basis_id, cotangent):
     vmem = pl.BlockSpec(memory_space=pltpu.VMEM)
-    smem = pl.BlockSpec(memory_space=pltpu.SMEM)
-    hbm = pl.BlockSpec(memory_space=pl.ANY)
+    hbm = pl.BlockSpec(memory_space=pltpu.HBM)
     dma = pltpu.SemaphoreType.DMA
     scratch = [
+        pltpu.VMEM((2, C, 2, LANES), BF),
+        pltpu.VMEM((C, 256), BF),
+        pltpu.VMEM((C, 256), BF),
+        pltpu.SMEM((K, 5, 16), F32),
+        pltpu.SMEM((2, N_ROWS), jnp.int32),
+        pltpu.SMEM((5, N_ROWS), jnp.int32),
         pltpu.VMEM((C, C * K), BF),
         pltpu.VMEM((2, C, 256), BF),
         pltpu.VMEM((16, C), BF),
@@ -400,7 +435,7 @@
         pltpu.VMEM((2, NZ, 16, LANES), BF),
         pltpu.VMEM((2, NZ, 16, LANES), BF),
         pltpu.VMEM((2, 4, 80, LANES), BF),
-        dma,
+        dma((6,)),
         dma((2, 2)), dma((2, 2)), dma((6,)), dma((6,)), dma((2,)), dma((2,)), dma((6,)), dma((6,)),
         dma((2,)), dma((2,)),
         dma((2, 4)), dma((2, 4)), dma((2, 4)), dma((2, 4)), dma((2, NZ)), dma((2, NZ)),
@@ -410,25 +445,25 @@
     out, ig, wg = pl.pallas_call(
         kernel,
         out_shape=(
-            jax.ShapeDtypeStruct((C, 256), BF),
-            jax.ShapeDtypeStruct((C, 256), BF),
-            jax.ShapeDtypeStruct((C, C * K), BF),
+            pltpu.VMEM((C, 2, LANES), BF),
+            pltpu.VMEM((C, 2, LANES), BF),
+            pltpu.VMEM((C, C * K), BF),
         ),
-        in_specs=[vmem, vmem, hbm, smem, smem, smem],
+        in_specs=[hbm] * 6,
         out_specs=(vmem, vmem, vmem),
         scratch_shapes=scratch,
         compiler_params=pltpu.CompilerParams(
-            collective_id=0, has_side_effects=True, vmem_limit_bytes=48 * 1024 * 1024
+            collective_id=0, has_side_effects=True, vmem_limit_bytes=56 * 1024 * 1024
         ),
     )(
-        features.reshape(C, 256),
-        cotangent.reshape(C, 256),
+        features,
+        cotangent,
         weight,
         filter_table.transpose(1, 2, 0),
         row_range.T,
         basis_id.T,
     )
-    return out.reshape(C, 2, LANES), ig.reshape(C, 2, LANES), wg.astype(F32)
+    return out, ig, wg.astype(F32)
 
 
 def solution(mesh):

time: 63 us -> 57.3 us (0.910)
  local copies, waits for them, and re-layouts: 5.78 us -> 1.31 us
  Pallas kernels: 54.7 us -> 53.7 us
    reshape x3 -> x0, local copies, waits for them, and re-layouts: 2.38 us -> none  [the longest x2 1.38 us: per_device(): return (out.reshape(C, 2, LANES), ig.reshape(C, 2, LANES), wg.astype(F32))]
    unnamed x8 -> x2, local copies, waits for them, and re-layouts: 3.4 us -> 1.31 us
    pallas_call x1, Pallas kernels: 54.7 us -> 53.7 us  [per_device(): pl.pallas_call(kernel, out_shape=(pltpu.VMEM((C, 2, LANES), BF), pltpu.VM...]
where the time goes in v3:
time: 57.3 us; the launch traced here: 57.2 us
  Pallas kernels  53.7 us (94%)
  other arithmetic  1.56 us (3%)
  local copies, waits for them, and re-layouts  1.31 us (2%)
  between operations  0.64 us (1%)
    pallas_call x1, Pallas kernels, per_device(): pl.pallas_call(kernel, out_shape=(pltpu.VMEM((C, 2, LANES), BF), pltpu.VM...  53.7 us
    convert_element_type x1, other arithmetic, per_device(): return (out, ig, wg.astype(F32))  1.56 us
    unnamed x2, local copies, waits for them, and re-layouts  1.31 us

profile of v3, /device:TPU:1, one launch (start us, length us, event | category | flops | bytes accessed | tf_op | source)
XLA Modules:
  0.0 57.2 jit_solution(2667884109809842951)
XLA Ops:
  0.6 53.7 %shard_map.85 = (bf16[256,2,128]{2,1,0:T(2,128)(2,1)S(1)}, bf16[256,2,128]{2,1,0:T(2,128)(2,1)S(1)}, bf16[256,2304]{1,0:T(8,128)(2,1)S(1)}) custom-call(bf16[256,2,128]{2,1,0:T(2,128)(2,1)} %feat_hbm.1, bf16[256,2,128]{2,1,0:T(2,128)(2,1)} %cot_hbm.1, bf16[256,2304]{1,0:T(8,128)(2,1)} %w_hbm.1, f32[9,5,16]{2,1,0:T(8,128)} %bitcast.3, s32[2,128]{1,0:T(2,128)} %bitcast.5, ...), custom_call_target="tpu_custom_call" | custom-call | tf_op jit(solution)/shard_map/pallas_call | solution.py:445
  54.3 0.7 %copy.11 = bf16[256,2,128]{2,1,0:T(2,128)(2,1)} copy(bf16[256,2,128]{2,1,0:T(2,128)(2,1)S(1)} %get-tuple-element.9) | data formatting | bytes 262144
  55.0 0.7 %copy.12 = bf16[256,2,128]{2,1,0:T(2,128)(2,1)} copy(bf16[256,2,128]{2,1,0:T(2,128)(2,1)S(1)} %get-tuple-element.10) | data formatting | bytes 262144
  55.6 1.6 %convert_element_type.3 = f32[256,2304]{1,0:T(8,128)} convert(bf16[256,2304]{1,0:T(8,128)(2,1)S(1)} %get-tuple-element.8) | non-fusion elementwise | flops 589824 | bytes 3538944 | tf_op jit(solution)/shard_map/convert_element_type | solution.py:466

commit v4 on v3

--- a/solution.py
+++ b/solution.py
@@ -32,10 +32,10 @@
     feat_hbm, cot_hbm, w_hbm, table_hbm, rng_hbm, ids_hbm,
     out, ig, wg,
     raw, feat, cot, table, rng, ids, w, fx, e_send, e_recv, bmat, bhal, big, bo, bgk, igp, gr, egs, egr,
-    cs, cr, own, s1, r1, zf, s2, r2, zg, s3, r3, g1, g2,
+    cs, cr, own, s1, r1, zf, s2, r2, zr, g2, wb, igo,
     in_sem, f_ss, f_rs, e_ss, e_rs, g_ss, g_rs, h_ss, h_rs, c_ss, c_rs,
-    s1_ss, s1_rs, s2_ss, s2_rs, s3_ss, s3_rs,
-    g1_ss, g1_rs, g2_ss, g2_rs, g3_ss, g3_rs, gc_ss, gc_rs,
+    s1_ss, s1_rs, s2_ss, s2_rs, z_ss, z_rs,
+    g2_ss, g2_rs, g3_ss, g3_rs, gc_ss, gc_rs,
 ):
     la, lo = lax.axis_index("lat"), lax.axis_index("lon")
     y, z, xh = la // 16, (la // 2) % 8, la % 2
@@ -228,19 +228,15 @@
         n = (me2[h] + i) % 4
         return remote(s2.at[h, n], r2.at[h, i], s2_ss.at[h, i], s2_rs.at[h, i], peer2[h](i))
 
-    def s3_copy(h, i):
-        n = (z + i) % 8
-        return remote(s3.at[h, n], r3.at[h, i], s3_ss.at[h, i], s3_rs.at[h, i], z_peer(i))
-
-    def g1_copy(h, i, n):
-        return remote(g1.at[h, n], g1.at[h, n], g1_ss.at[h, i], g1_rs.at[h, i], z_peer(i))
+    def z_copy(h, i, n):
+        return remote(zr.at[h, n], zr.at[h, n], z_ss.at[h, i], z_rs.at[h, i], z_peer(i))
 
     def g2_copy(h, i, n):
         return remote(g2.at[h, n], g2.at[h, n], g2_ss.at[h, i], g2_rs.at[h, i], peer2[h](i))
 
     def piece(h, c, n):
         rows = pl.ds(pl.multiple_of(128 * c + 32 * n, 32), 32)
-        return wg.at[rows, h * HALF : (h + 1) * HALF]
+        return wb.at[rows, h * HALF : (h + 1) * HALF]
 
     def g3_copy(h, i, n):
         ref = piece(h, core, n)
@@ -274,29 +270,20 @@
         for i in (1, 2, 3):
             s2_copy(h, i).wait()
             total += r2[h, i].astype(F32)
-        zg[h] = total
-        for i in range(NZ):
-            s3[h, i] = zg[h, 9 * i : 9 * i + 16, :].astype(BF)
+        zr[h, z] = total.astype(BF)
+        for i in (4, 3, 5, 2, 6, 1, 7):
+            z_copy(h, i, z).start()
+
+    def sum_z(h):
         for i in range(1, NZ):
-            s3_copy(h, i).start()
-
-    def sum3(h):
-        total = s3[h, z].astype(F32)
+            z_copy(h, i, z).wait_send()
+            z_copy(h, i, (z + 8 - i) % 8).wait_recv()
+        total = zr[h, 0].astype(F32)
         for i in range(1, NZ):
-            s3_copy(h, i).wait()
-            total += r3[h, i].astype(F32)
-        g1[h, z] = (total * F32(1.0 / math.sqrt(N_ROWS * N_LON * LANES))).astype(BF)
-        for i in range(1, NZ):
-            g1_copy(h, i, z).start()
-
-    def gather1(h):
-        for i in range(1, NZ):
-            g1_copy(h, i, z).wait_send()
-            g1_copy(h, i, (z + 8 - i) % 8).wait_recv()
-        for i in range(NZ):
-            zg[h, 9 * i : 9 * i + 16, :] = g1[h, i].astype(F32)
-        g2[h, me2[h]] = zg[h].astype(BF)
-        for i in (1, 2, 3):
+            total += zr[h, i].astype(F32)
+        total *= F32(1.0 / math.sqrt(N_ROWS * N_LON * LANES))
+        g2[h, me2[h]] = total.astype(BF)
+        for i in (2, 1, 3):
             g2_copy(h, i, me2[h]).start()
 
     def gather2(h):
@@ -307,24 +294,36 @@
         rows = pl.ds(pl.multiple_of(128 * core + 32 * me1[h], 32), 32)
         for m in range(TILES):
             a = h * HALF + m * LANES
-            wg[rows, a : a + LANES] = zf[h, :, 8 * m : 8 * m + 8, :].reshape(32, LANES).astype(BF)
-        for i in (1, 2, 3):
+            wb[rows, a : a + LANES] = zf[h, :, 8 * m : 8 * m + 8, :].reshape(32, LANES).astype(BF)
+        for i in (2, 1, 3):
             g3_copy(h, i, me1[h]).start()
         gc_copy(h, 0, core, me1[h]).start()
+        widen(h, core, me1[h])
+
+    def widen(h, c, n):
+        rows = pl.ds(pl.multiple_of(128 * c + 32 * n, 32), 32)
+        cols = slice(h * HALF, (h + 1) * HALF)
+        wg[rows, cols] = wb[rows, cols].astype(F32)
 
     def gather3(h, i):
         n = (me1[h] + 4 - i) % 4
         g3_copy(h, i, n).wait_recv()
         gc_copy(h, i, core, n).start()
+        widen(h, core, n)
+
+    def gather_core(h, i):
+        n = (me1[h] + 4 - i) % 4
+        gc_copy(h, i, 1 - core, n).wait_recv()
+        widen(h, 1 - core, n)
 
     for c in feat_copies[0] + edge_copies:
         c.wait()
     basis(0)
     weight_rows(0)
+    core_sum(0)
     for c in feat_copies[1]:
         c.wait()
     basis(1)
-    core_sum(0)
     weight_rows(1)
     core_sum(1)
 
@@ -333,6 +332,7 @@
     for m in range(1, K):
         acc += dot(w[:, m * 256 : m * 256 + 256], bo[m * 256 : m * 256 + 256, :])
     out[...] = lanes_to_rows(acc)
+    sum1(0)
 
     def basis_grad(m, _):
         cols = pl.ds(pl.multiple_of(m * 256, 256), 256)
@@ -342,13 +342,11 @@
         return 0
 
     lax.fori_loop(0, K, basis_grad, 0)
-    sum1(0)
     sum1(1)
     for k in range(K):
         for t in range(2):
             bgk[k, :, t * LANES : (t + 1) * LANES] = big[t, pl.ds(k, C, stride=K), :].astype(BF)
     sum2(0)
-    sum2(1)
 
     def input_grad(dl):
         acc = dot(bgk[0], bmat[0, dl], NT)
@@ -357,6 +355,7 @@
         return acc
 
     igp[0] = input_grad(0).astype(BF)
+    sum2(1)
     igp[1] = input_grad(2).astype(BF)
     acc = dot(bhal[0], bgk[0], NT)
     for k in range(1, K):
@@ -369,10 +368,9 @@
     ] + [remote(egs.at[s], egr.at[s], h_ss.at[s], h_rs.at[s], edge_peer(s)) for s in range(6)]
     for c in grad_copies:
         c.start()
-    sum3(0)
-    sum3(1)
-    gather1(0)
-    gather1(1)
+    igo[...] = input_grad(1)
+    sum_z(0)
+    sum_z(1)
     gather2(0)
     gather2(1)
 
@@ -381,21 +379,36 @@
     edges = egr[0].astype(F32)
     for s in range(1, 6):
         edges += egr[s].astype(F32)
-    acc = input_grad(1) + gr[0].astype(F32) + gr[1].astype(F32)
+    acc = igo[...] + gr[0].astype(F32) + gr[1].astype(F32)
     edge_hi = edges.astype(BF)
     edge_lo = (edges - edge_hi.astype(F32)).astype(BF)
     acc += dot(edge_hi, sel, TN) + dot(edge_lo, sel, TN)
     ig[...] = lanes_to_rows(acc)
 
-    for i in (1, 3, 2):
-        for h in range(2):
+    for h in range(2):
+        for i in (1, 3, 2):
             gather3(h, i)
+    for h in range(2):
+        for i in (0, 1, 3, 2):
+            gather_core(h, i)
     for h in range(2):
         for i in range(4):
             gc_copy(h, i, core, (me1[h] + 4 - i) % 4).wait_send()
-            gc_copy(h, i, 1 - core, (me1[h] + 4 - i) % 4).wait_recv()
         for i in (1, 2, 3):
             g3_copy(h, i, me1[h]).wait_send()
+
+
+def write_back(out_v, ig_v, wg_v, out, ig, wg, sem):
+    copies = [
+        pltpu.make_async_copy(wg_v.at[n : n + 64], wg.at[n : n + 64], sem.at[n // 64])
+        for n in range(0, C, 64)
+    ]
+    copies.append(pltpu.make_async_copy(out_v, out, sem.at[4]))
+    copies.append(pltpu.make_async_copy(ig_v, ig, sem.at[5]))
+    for c in copies:
+        c.start()
+    for c in copies:
+        c.wait()
 
 
 def per_device(features, weight, filter_table, row_range, basis_id, cotangent):
@@ -430,24 +443,22 @@
         pltpu.VMEM((2, 4, 80, LANES), F32),
         pltpu.VMEM((2, 4, 80, LANES), BF),
         pltpu.VMEM((2, 4, 80, LANES), BF),
-        pltpu.VMEM((2, 80, LANES), F32),
-        pltpu.VMEM((2, NZ, 16, LANES), BF),
-        pltpu.VMEM((2, NZ, 16, LANES), BF),
-        pltpu.VMEM((2, NZ, 16, LANES), BF),
+        pltpu.VMEM((2, NZ, 80, LANES), BF),
         pltpu.VMEM((2, 4, 80, LANES), BF),
+        pltpu.VMEM((C, C * K), BF),
+        pltpu.VMEM((C, 256), F32),
         dma((6,)),
         dma((2, 2)), dma((2, 2)), dma((6,)), dma((6,)), dma((2,)), dma((2,)), dma((6,)), dma((6,)),
         dma((2,)), dma((2,)),
         dma((2, 4)), dma((2, 4)), dma((2, 4)), dma((2, 4)), dma((2, NZ)), dma((2, NZ)),
-        dma((2, NZ)), dma((2, NZ)), dma((2, 4)), dma((2, 4)), dma((2, 4)), dma((2, 4)),
-        dma((2, 4)), dma((2, 4)),
+        dma((2, 4)), dma((2, 4)), dma((2, 4)), dma((2, 4)), dma((2, 4)), dma((2, 4)),
     ]
     out, ig, wg = pl.pallas_call(
         kernel,
         out_shape=(
             pltpu.VMEM((C, 2, LANES), BF),
             pltpu.VMEM((C, 2, LANES), BF),
-            pltpu.VMEM((C, C * K), BF),
+            pltpu.VMEM((C, C * K), F32),
         ),
         in_specs=[hbm] * 6,
         out_specs=(vmem, vmem, vmem),
@@ -463,7 +474,17 @@
         row_range.T,
         basis_id.T,
     )
-    return out, ig, wg.astype(F32)
+    return pl.pallas_call(
+        write_back,
+        out_shape=(
+            jax.ShapeDtypeStruct((C, 2, LANES), BF),
+            jax.ShapeDtypeStruct((C, 2, LANES), BF),
+            jax.ShapeDtypeStruct((C, C * K), F32),
+        ),
+        in_specs=[vmem] * 3,
+        out_specs=(hbm, hbm, hbm),
+        scratch_shapes=[dma((6,))],
+    )(*[pltpu.with_memory_space_constraint(v, pltpu.VMEM) for v in (out, ig, wg)])
 
 
 def solution(mesh):

time: 57.3 us -> 55.2 us (0.963); the launches traced: 57.2 us -> 54.5 us
  other arithmetic: 1.56 us -> 0 us
  local copies, waits for them, and re-layouts: 1.31 us -> 0 us
    convert_element_type x1 -> x0, other arithmetic: 1.56 us -> none  [per_device(): return (out, ig, wg.astype(F32))]
    pallas_call x0 -> x1, Pallas kernels: none -> 1.53 us  [per_device(): pl.pallas_call(write_back, out_shape=(jax.ShapeDtypeStruct((C, 2, LANES),...]
    pallas_call x1, Pallas kernels: 53.7 us -> 52.3 us  [per_device(): pl.pallas_call(kernel, out_shape=(pltpu.VMEM((C, 2, LANES), BF), pltpu.VM...]
    unnamed x2 -> x0, local copies, waits for them, and re-layouts: 1.31 us -> none
where the time goes in v4:
time: 55.2 us; the launch traced here: 54.5 us
  Pallas kernels  53.8 us (97%)
  between operations  0.64 us (1%)
    pallas_call x1, Pallas kernels, per_device(): pl.pallas_call(kernel, out_shape=(pltpu.VMEM((C, 2, LANES), BF), pltpu.VM...  52.3 us
    pallas_call x1, Pallas kernels, per_device(): pl.pallas_call(write_back, out_shape=(jax.ShapeDtypeStruct((C, 2, LANES),...  1.53 us

profile of v4, /device:TPU:1, one launch (start us, length us, event | category | flops | bytes accessed | tf_op | source)
XLA Modules:
  0.0 54.5 jit_solution(11963672592635690407)
XLA Ops:
  0.6 52.3 %shard_map.85 = (bf16[256,2,128]{2,1,0:T(2,128)(2,1)S(1)}, bf16[256,2,128]{2,1,0:T(2,128)(2,1)S(1)}, f32[256,2304]{1,0:T(8,128)S(1)}) custom-call(bf16[256,2,128]{2,1,0:T(2,128)(2,1)} %feat_hbm.1, bf16[256,2,128]{2,1,0:T(2,128)(2,1)} %cot_hbm.1, bf16[256,2304]{1,0:T(8,128)(2,1)} %w_hbm.1, f32[9,5,16]{2,1,0:T(8,128)} %bitcast.3, s32[2,128]{1,0:T(2,128)} %bitcast.5, ...), custom_call_target="tpu_custom_call" | custom-call | tf_op jit(solution)/shard_map/pallas_call | solution.py:456
  53.0 1.5 %shard_map.86 = (bf16[256,2,128]{2,1,0:T(2,128)(2,1)}, bf16[256,2,128]{2,1,0:T(2,128)(2,1)}, f32[256,2304]{1,0:T(8,128)}) custom-call(bf16[256,2,128]{2,1,0:T(2,128)(2,1)S(1)} %get-tuple-element.6.out_v, bf16[256,2,128]{2,1,0:T(2,128)(2,1)S(1)} %get-tuple-element.7.ig_v, f32[256,2304]{1,0:T(8,128)S(1)} %get-tuple-element.8.wg_v), custom_call_target="tpu_custom_call" | custom-call | tf_op jit(solution)/shard_map/pallas_call | solution.py:477

commit v5 on v4

--- a/solution.py
+++ b/solution.py
@@ -17,8 +17,11 @@
 NZ = 8
 N_LAT, N_LON = 64, 4
 N_ROWS = 128
-HALF = C * K // 2
-TILES = HALF // LANES
+CHANNELS = [(0, 144), (144, 256)]
+COLUMNS = [(0, 1280), (1280, 2304)]
+PIECE = [slice(0, 80), slice(80, 144)]
+NEAR_FIRST = [1, 3, 4, 12, 5, 7, 13, 15, 2, 8, 6, 14, 9, 11, 10]
+Z_FAR_FIRST = [4, 3, 5, 2, 6, 1, 7]
 NT = (((1,), (1,)), ((), ()))
 TN = (((0,), (0,)), ((), ()))
 NN = (((1,), (0,)), ((), ()))
@@ -31,18 +34,17 @@
 def kernel(
     feat_hbm, cot_hbm, w_hbm, table_hbm, rng_hbm, ids_hbm,
     out, ig, wg,
-    raw, feat, cot, table, rng, ids, w, fx, e_send, e_recv, bmat, bhal, big, bo, bgk, igp, gr, egs, egr,
-    cs, cr, own, s1, r1, zf, s2, r2, zr, g2, wb, igo,
+    raw, feat, cot, table, rng, ids, w, fx, e_send, e_recv, e_rows, bmat, bhal, big, bo, bgk, igp, gr, egs, egr,
+    cs, cr, own, xs, xr, zr, ga, igo,
     in_sem, f_ss, f_rs, e_ss, e_rs, g_ss, g_rs, h_ss, h_rs, c_ss, c_rs,
-    s1_ss, s1_rs, s2_ss, s2_rs, z_ss, z_rs,
-    g2_ss, g2_rs, g3_ss, g3_rs, gc_ss, gc_rs,
+    x_ss, x_rs, z_ss, z_rs, gx_ss, gx_rs, gc_ss, gc_rs,
 ):
     la, lo = lax.axis_index("lat"), lax.axis_index("lon")
     y, z, xh = la // 16, (la // 2) % 8, la % 2
     xl, core = lo // 2, lo % 2
     x = xh * 2 + xl
     sibling = (la, lo + 1 - 2 * core)
-    me1, me2 = (y, x), (x, y)
+    me_n = y * 4 + x
 
     def lat_peer(dl):
         return (lax.rem(la + dl + N_LAT, N_LAT), lo)
@@ -51,17 +53,23 @@
         dl, dc = s // 2 - 1, 2 * (s % 2) - 1
         return (lax.rem(la + dl + N_LAT, N_LAT), lax.rem(lo + dc + N_LON, N_LON))
 
-    def y_peer(i):
-        return ((((y + i) % 4) * 8 + z) * 2 + xh, lo)
-
-    def x_peer(i):
-        px = (x + i) % 4
-        return ((y * 8 + z) * 2 + px // 2, (px % 2) * 2 + core)
+    def plane(i, sign=1):
+        return (y + 4 + sign * (i // 4)) % 4, (x + 4 + sign * (i % 4)) % 4
+
+    def xy_peer(i):
+        py, px = plane(i)
+        return ((py * 8 + z) * 2 + px // 2, (px % 2) * 2 + core)
+
+    def xy_index(i):
+        py, px = plane(i)
+        return py * 4 + px
+
+    def from_index(i):
+        py, px = plane(i, -1)
+        return py * 4 + px
 
     def z_peer(i):
         return ((y * 8 + (z + i) % 8) * 2 + xh, lo)
-
-    peer1, peer2 = (y_peer, x_peer), (x_peer, y_peer)
 
     in_copies = [
         pltpu.make_async_copy(src, dst, in_sem.at[i])
@@ -81,7 +89,7 @@
 
     barrier = pltpu.get_barrier_semaphore()
     peers = [lat_peer(-1), lat_peer(1)] + [edge_peer(s) for s in range(6)]
-    peers += [y_peer(i) for i in (1, 2, 3)] + [x_peer(i) for i in (1, 3)]
+    peers += [xy_peer(i) for i in NEAR_FIRST if i != 2]
     peers += [z_peer(i) for i in range(1, NZ)]
     for peer in peers:
         pl.semaphore_signal(barrier, inc=1, device_id=peer, device_id_type=MESH)
@@ -111,7 +119,7 @@
             src_ref=src, dst_ref=dst, send_sem=ss, recv_sem=rs, device_id=peer, device_id_type=MESH
         )
 
-    half_rows = [slice(0, 128), slice(128, 256)]
+    half_rows = [slice(*c) for c in CHANNELS]
     feat_copies = [
         [
             remote(
@@ -126,7 +134,7 @@
     edge_copies = [
         remote(e_send, e_recv.at[5 - s], e_ss.at[s], e_rs.at[5 - s], edge_peer(s)) for s in range(6)
     ]
-    for c in feat_copies[0] + edge_copies + feat_copies[1]:
+    for c in feat_copies[0] + edge_copies:
         c.start()
 
     for c in in_copies[1:4]:
@@ -186,138 +194,125 @@
                 bhal[k, s * 16 : s * 16 + 16, lanes] = v.astype(BF)
         return 0
 
-    lax.fori_loop(0, K, build, 0)
-    for h in range(2):
-        zf[h, :, 72:80, :] = jnp.zeros((4, 8, LANES), F32)
+    lax.fori_loop(0, 4, build, 0)
+    for c in feat_copies[0]:
+        c.wait_send()
+    for c in feat_copies[1]:
+        c.start()
+    lax.fori_loop(4, K, build, 0)
 
     in_copies[4].wait()
     rows_to_lanes(raw.at[1], cot)
 
     theirs = pl.ds(pl.multiple_of(128 * (1 - core), 128), 128)
     mine = pl.ds(pl.multiple_of(128 * core, 128), 128)
-    chunks = [(0, 256), (256, 512), (512, 768), (768, 1024), (1024, 1152)]
 
     def core_copy(h):
-        return remote(cs.at[h], cr.at[h], c_ss.at[h], c_rs.at[h], sibling)
+        cols = slice(*COLUMNS[h])
+        return remote(cs.at[:, cols], cr.at[:, cols], c_ss.at[h], c_rs.at[h], sibling)
 
     def basis(h):
         hc = half_rows[h]
-        halo = e_recv[:, :, hc].reshape(96, 128)
         for k in range(K):
             acc = dot(feat[hc, :], bmat[k, 1]) + dot(fx[0, hc, :], bmat[k, 0])
-            acc += dot(fx[1, hc, :], bmat[k, 2]) + dot(halo, bhal[k], TN)
-            rows = pl.ds(h * HALF + k, 128, stride=K)
+            acc += dot(fx[1, hc, :], bmat[k, 2]) + dot(e_rows[hc, :], bhal[k])
+            rows = pl.ds(hc.start * K + k, hc.stop - hc.start, stride=K)
             big[0, rows, :] = acc[:, :LANES]
             big[1, rows, :] = acc[:, LANES:]
-        for a, b in chunks:
-            rows = slice(h * HALF + a, h * HALF + b)
+        for a in range(*COLUMNS[h], 256):
+            rows = slice(a, a + 256)
             bo[rows, :LANES] = big[0, rows, :].astype(BF)
             bo[rows, LANES:] = big[1, rows, :].astype(BF)
-            cs[h, :, a:b] = dot(cot[theirs, :], bo[rows, :], NT).astype(BF)
+            cs[:, rows] = dot(cot[theirs, :], bo[rows, :], NT).astype(BF)
         core_copy(h).start()
 
     def weight_rows(h):
-        for a, b in chunks:
-            own[h, :, a:b] = dot(cot[mine, :], bo[h * HALF + a : h * HALF + b, :], NT)
-
-    def s1_copy(h, i):
-        rows = pl.ds(pl.multiple_of(32 * ((me1[h] + i) % 4), 32), 32)
-        return remote(s1.at[h, rows], r1.at[h, i], s1_ss.at[h, i], s1_rs.at[h, i], peer1[h](i))
-
-    def s2_copy(h, i):
-        n = (me2[h] + i) % 4
-        return remote(s2.at[h, n], r2.at[h, i], s2_ss.at[h, i], s2_rs.at[h, i], peer2[h](i))
+        for a in range(*COLUMNS[h], 256):
+            own[:, a : a + 256] = dot(cot[mine, :], bo[a : a + 256, :], NT)
+
+    def xy_copy(h, i):
+        src, dst = xs.at[xy_index(i), PIECE[h]], xr.at[i, PIECE[h]]
+        return remote(src, dst, x_ss.at[h, i], x_rs.at[h, i], xy_peer(i))
 
     def z_copy(h, i, n):
-        return remote(zr.at[h, n], zr.at[h, n], z_ss.at[h, i], z_rs.at[h, i], z_peer(i))
-
-    def g2_copy(h, i, n):
-        return remote(g2.at[h, n], g2.at[h, n], g2_ss.at[h, i], g2_rs.at[h, i], peer2[h](i))
-
-    def piece(h, c, n):
-        rows = pl.ds(pl.multiple_of(128 * c + 32 * n, 32), 32)
-        return wb.at[rows, h * HALF : (h + 1) * HALF]
-
-    def g3_copy(h, i, n):
-        ref = piece(h, core, n)
-        return remote(ref, ref, g3_ss.at[h, i], g3_rs.at[h, i], peer1[h](i))
-
-    def gc_copy(h, i, c, n):
-        ref = piece(h, c, n)
+        ref = zr.at[n, PIECE[h]]
+        return remote(ref, ref, z_ss.at[h, i], z_rs.at[h, i], z_peer(i))
+
+    def gx_copy(h, i, n):
+        ref = ga.at[core, n, PIECE[h]]
+        return remote(ref, ref, gx_ss.at[h, i], gx_rs.at[h, i], xy_peer(i))
+
+    def gc_copy(h, i, c):
+        ref = ga.at[c, from_index(i), PIECE[h]]
         return remote(ref, ref, gc_ss.at[h, i], gc_rs.at[h, i], sibling)
+
+    def sent(copy, order, *args):
+        for i in order:
+            copy(0, i, *args).wait_send()
 
     def core_sum(h):
         core_copy(h).wait()
-        s1[h] = (own[h] + cr[h].astype(F32)).astype(BF)
-        for i in (1, 2, 3):
-            s1_copy(h, i).start()
-
-    def sum1(h):
-        rows = pl.ds(pl.multiple_of(32 * me1[h], 32), 32)
-        total = s1[h, rows, :].astype(F32)
-        for i in (1, 2, 3):
-            s1_copy(h, i).wait()
-            total += r1[h, i].astype(F32)
-        for m in range(TILES):
-            tile = total[:, m * LANES : (m + 1) * LANES]
-            zf[h, :, 8 * m : 8 * m + 8, :] = tile.reshape(4, 8, LANES)
-        s2[h] = zf[h].astype(BF)
-        for i in (1, 2, 3):
-            s2_copy(h, i).start()
-
-    def sum2(h):
-        total = s2[h, me2[h]].astype(F32)
-        for i in (1, 2, 3):
-            s2_copy(h, i).wait()
-            total += r2[h, i].astype(F32)
-        zr[h, z] = total.astype(BF)
-        for i in (4, 3, 5, 2, 6, 1, 7):
+        cols = slice(*COLUMNS[h])
+        v = own[:, cols] + cr[:, cols].astype(F32)
+        tiles = [v[:, a : a + LANES].reshape(16, 8, LANES) for a in range(0, v.shape[1], LANES)]
+        for m in range(0, len(tiles), 2):
+            rows = slice(PIECE[h].start + 8 * m, PIECE[h].start + 8 * m + 16)
+            xs[:, rows, :] = jnp.concatenate(tiles[m : m + 2], axis=1).astype(BF)
+        if h == 1:
+            sent(xy_copy, NEAR_FIRST)
+        for i in reversed(NEAR_FIRST):
+            xy_copy(h, i).start()
+
+    def sum_xy(h):
+        total = xs[me_n, PIECE[h], :].astype(F32)
+        for i in NEAR_FIRST:
+            xy_copy(h, i).wait_recv()
+            total += xr[i, PIECE[h], :].astype(F32)
+        zr[z, PIECE[h], :] = total.astype(BF)
+        if h == 1:
+            sent(z_copy, Z_FAR_FIRST, z)
+        for i in Z_FAR_FIRST:
             z_copy(h, i, z).start()
 
     def sum_z(h):
         for i in range(1, NZ):
-            z_copy(h, i, z).wait_send()
             z_copy(h, i, (z + 8 - i) % 8).wait_recv()
-        total = zr[h, 0].astype(F32)
+        total = zr[0, PIECE[h], :].astype(F32)
         for i in range(1, NZ):
-            total += zr[h, i].astype(F32)
+            total += zr[i, PIECE[h], :].astype(F32)
         total *= F32(1.0 / math.sqrt(N_ROWS * N_LON * LANES))
-        g2[h, me2[h]] = total.astype(BF)
-        for i in (2, 1, 3):
-            g2_copy(h, i, me2[h]).start()
-
-    def gather2(h):
-        for i in (1, 2, 3):
-            g2_copy(h, i, me2[h]).wait_send()
-            g2_copy(h, i, (me2[h] + 4 - i) % 4).wait_recv()
-        zf[h] = g2[h].astype(F32)
-        rows = pl.ds(pl.multiple_of(128 * core + 32 * me1[h], 32), 32)
-        for m in range(TILES):
-            a = h * HALF + m * LANES
-            wb[rows, a : a + LANES] = zf[h, :, 8 * m : 8 * m + 8, :].reshape(32, LANES).astype(BF)
-        for i in (2, 1, 3):
-            g3_copy(h, i, me1[h]).start()
-        gc_copy(h, 0, core, me1[h]).start()
-        widen(h, core, me1[h])
+        ga[core, me_n, PIECE[h], :] = total.astype(BF)
+        gc_copy(h, 0, core).start()
+        if h == 1:
+            sent(gx_copy, NEAR_FIRST, me_n)
+        for i in reversed(NEAR_FIRST):
+            gx_copy(h, i, me_n).start()
+        widen(h, core, me_n)
 
     def widen(h, c, n):
-        rows = pl.ds(pl.multiple_of(128 * c + 32 * n, 32), 32)
-        cols = slice(h * HALF, (h + 1) * HALF)
-        wg[rows, cols] = wb[rows, cols].astype(F32)
-
-    def gather3(h, i):
-        n = (me1[h] + 4 - i) % 4
-        g3_copy(h, i, n).wait_recv()
-        gc_copy(h, i, core, n).start()
-        widen(h, core, n)
-
-    def gather_core(h, i):
-        n = (me1[h] + 4 - i) % 4
-        gc_copy(h, i, 1 - core, n).wait_recv()
-        widen(h, 1 - core, n)
-
-    for c in feat_copies[0] + edge_copies:
+        v = ga[c, n, PIECE[h], :].astype(F32)
+        rows = pl.ds(pl.multiple_of(128 * c + 8 * n, 8), 8)
+        for m in range(v.shape[0] // 8):
+            a = COLUMNS[h][0] + m * LANES
+            wg[rows, a : a + LANES] = v[8 * m : 8 * m + 8]
+
+    def gather_xy(h):
+        for i in NEAR_FIRST:
+            n = from_index(i)
+            gx_copy(h, i, n).wait_recv()
+            gc_copy(h, i, core).start()
+            widen(h, core, n)
+
+    def gather_core(h):
+        for i in [0] + NEAR_FIRST:
+            gc_copy(h, i, 1 - core).wait_recv()
+            widen(h, 1 - core, from_index(i))
+
+    for c in feat_copies[0]:
+        c.wait_recv()
+    for c in edge_copies:
         c.wait()
+    e_rows[...] = jnp.transpose(e_recv[...].reshape(96, C).astype(F32)).astype(BF)
     basis(0)
     weight_rows(0)
     core_sum(0)
@@ -328,11 +323,6 @@
     core_sum(1)
 
     in_copies[5].wait()
-    acc = dot(w[:, :256], bo[:256, :])
-    for m in range(1, K):
-        acc += dot(w[:, m * 256 : m * 256 + 256], bo[m * 256 : m * 256 + 256, :])
-    out[...] = lanes_to_rows(acc)
-    sum1(0)
 
     def basis_grad(m, _):
         cols = pl.ds(pl.multiple_of(m * 256, 256), 256)
@@ -342,11 +332,9 @@
         return 0
 
     lax.fori_loop(0, K, basis_grad, 0)
-    sum1(1)
     for k in range(K):
         for t in range(2):
             bgk[k, :, t * LANES : (t + 1) * LANES] = big[t, pl.ds(k, C, stride=K), :].astype(BF)
-    sum2(0)
 
     def input_grad(dl):
         acc = dot(bgk[0], bmat[0, dl], NT)
@@ -355,7 +343,7 @@
         return acc
 
     igp[0] = input_grad(0).astype(BF)
-    sum2(1)
+    sum_xy(0)
     igp[1] = input_grad(2).astype(BF)
     acc = dot(bhal[0], bgk[0], NT)
     for k in range(1, K):
@@ -369,10 +357,15 @@
     for c in grad_copies:
         c.start()
     igo[...] = input_grad(1)
+    sum_xy(1)
+
+    acc = dot(w[:, :256], bo[:256, :])
+    for m in range(1, K):
+        acc += dot(w[:, m * 256 : m * 256 + 256], bo[m * 256 : m * 256 + 256, :])
+    out[...] = lanes_to_rows(acc)
     sum_z(0)
     sum_z(1)
-    gather2(0)
-    gather2(1)
+    gather_xy(0)
 
     for c in grad_copies:
         c.wait()
@@ -385,17 +378,17 @@
     acc += dot(edge_hi, sel, TN) + dot(edge_lo, sel, TN)
     ig[...] = lanes_to_rows(acc)
 
+    gather_core(0)
+    gather_xy(1)
+    gather_core(1)
+    for i in NEAR_FIRST:
+        xy_copy(1, i).wait_send()
+        gx_copy(1, i, me_n).wait_send()
+    for i in Z_FAR_FIRST:
+        z_copy(1, i, z).wait_send()
     for h in range(2):
-        for i in (1, 3, 2):
-            gather3(h, i)
-    for h in range(2):
-        for i in (0, 1, 3, 2):
-            gather_core(h, i)
-    for h in range(2):
-        for i in range(4):
-            gc_copy(h, i, core, (me1[h] + 4 - i) % 4).wait_send()
-        for i in (1, 2, 3):
-            g3_copy(h, i, me1[h]).wait_send()
+        for i in [0] + NEAR_FIRST:
+            gc_copy(h, i, core).wait_send()
 
 
 def write_back(out_v, ig_v, wg_v, out, ig, wg, sem):
@@ -426,6 +419,7 @@
         pltpu.VMEM((2, C, 256), BF),
         pltpu.VMEM((16, C), BF),
         pltpu.VMEM((6, 16, C), BF),
+        pltpu.VMEM((C, 96), BF),
         pltpu.VMEM((K, 3, 256, 256), BF),
         pltpu.VMEM((K, 96, 256), BF),
         pltpu.VMEM((2, C * K, LANES), F32),
@@ -435,23 +429,19 @@
         pltpu.VMEM((2, C, 256), BF),
         pltpu.VMEM((6, 16, C), BF),
         pltpu.VMEM((6, 16, C), BF),
-        pltpu.VMEM((2, 128, HALF), BF),
-        pltpu.VMEM((2, 128, HALF), BF),
-        pltpu.VMEM((2, 128, HALF), F32),
-        pltpu.VMEM((2, 128, HALF), BF),
-        pltpu.VMEM((2, 4, 32, HALF), BF),
-        pltpu.VMEM((2, 4, 80, LANES), F32),
-        pltpu.VMEM((2, 4, 80, LANES), BF),
-        pltpu.VMEM((2, 4, 80, LANES), BF),
-        pltpu.VMEM((2, NZ, 80, LANES), BF),
-        pltpu.VMEM((2, 4, 80, LANES), BF),
-        pltpu.VMEM((C, C * K), BF),
+        pltpu.VMEM((128, C * K), BF),
+        pltpu.VMEM((128, C * K), BF),
+        pltpu.VMEM((128, C * K), F32),
+        pltpu.VMEM((16, 144, LANES), BF),
+        pltpu.VMEM((16, 144, LANES), BF),
+        pltpu.VMEM((NZ, 144, LANES), BF),
+        pltpu.VMEM((2, 16, 144, LANES), BF),
         pltpu.VMEM((C, 256), F32),
         dma((6,)),
         dma((2, 2)), dma((2, 2)), dma((6,)), dma((6,)), dma((2,)), dma((2,)), dma((6,)), dma((6,)),
         dma((2,)), dma((2,)),
-        dma((2, 4)), dma((2, 4)), dma((2, 4)), dma((2, 4)), dma((2, NZ)), dma((2, NZ)),
-        dma((2, 4)), dma((2, 4)), dma((2, 4)), dma((2, 4)), dma((2, 4)), dma((2, 4)),
+        dma((2, 16)), dma((2, 16)), dma((2, NZ)), dma((2, NZ)),
+        dma((2, 16)), dma((2, 16)), dma((2, 16)), dma((2, 16)),
     ]
     out, ig, wg = pl.pallas_call(
         kernel,

time: 55.2 us -> 52.3 us (0.947); the launches traced: 54.5 us -> 52.2 us
  Pallas kernels: 53.8 us -> 51.6 us
    pallas_call x1, Pallas kernels: 52.3 us -> 50.1 us  [per_device(): pl.pallas_call(kernel, out_shape=(pltpu.VMEM((C, 2, LANES), BF), pltpu.VM...]
where the time goes in v5:
time: 52.3 us; the launch traced here: 52.2 us
  Pallas kernels  51.6 us (99%)
  between operations  0.64 us (1%)
    pallas_call x1, Pallas kernels, per_device(): pl.pallas_call(kernel, out_shape=(pltpu.VMEM((C, 2, LANES), BF), pltpu.VM...  50.1 us
    pallas_call x1, Pallas kernels, per_device(): pl.pallas_call(write_back, out_shape=(jax.ShapeDtypeStruct((C, 2, LANES),...  1.53 us

profile of v5, /device:TPU:1, one launch (start us, length us, event | category | flops | bytes accessed | tf_op | source)
XLA Modules:
  0.0 52.2 jit_solution(6570829242024177045)
XLA Ops:
  0.6 50.1 %shard_map.85 = (bf16[256,2,128]{2,1,0:T(2,128)(2,1)S(1)}, bf16[256,2,128]{2,1,0:T(2,128)(2,1)S(1)}, f32[256,2304]{1,0:T(8,128)S(1)}) custom-call(bf16[256,2,128]{2,1,0:T(2,128)(2,1)} %feat_hbm.1, bf16[256,2,128]{2,1,0:T(2,128)(2,1)} %cot_hbm.1, bf16[256,2304]{1,0:T(8,128)(2,1)} %w_hbm.1, f32[9,5,16]{2,1,0:T(8,128)} %bitcast.3, s32[2,128]{1,0:T(2,128)} %bitcast.5, ...), custom_call_target="tpu_custom_call" | custom-call | tf_op jit(solution)/shard_map/pallas_call | solution.py:446
  50.7 1.5 %shard_map.86 = (bf16[256,2,128]{2,1,0:T(2,128)(2,1)}, bf16[256,2,128]{2,1,0:T(2,128)(2,1)}, f32[256,2304]{1,0:T(8,128)}) custom-call(bf16[256,2,128]{2,1,0:T(2,128)(2,1)S(1)} %get-tuple-element.6.out_v, bf16[256,2,128]{2,1,0:T(2,128)(2,1)S(1)} %get-tuple-element.7.ig_v, f32[256,2304]{1,0:T(8,128)S(1)} %get-tuple-element.8.wg_v), custom_call_target="tpu_custom_call" | custom-call | tf_op jit(solution)/shard_map/pallas_call | solution.py:467

commit v6 on v5

--- a/solution.py
+++ b/solution.py
@@ -258,8 +258,6 @@
         for m in range(0, len(tiles), 2):
             rows = slice(PIECE[h].start + 8 * m, PIECE[h].start + 8 * m + 16)
             xs[:, rows, :] = jnp.concatenate(tiles[m : m + 2], axis=1).astype(BF)
-        if h == 1:
-            sent(xy_copy, NEAR_FIRST)
         for i in reversed(NEAR_FIRST):
             xy_copy(h, i).start()
 
@@ -382,6 +380,7 @@
     gather_xy(1)
     gather_core(1)
     for i in NEAR_FIRST:
+        xy_copy(0, i).wait_send()
         xy_copy(1, i).wait_send()
         gx_copy(1, i, me_n).wait_send()
     for i in Z_FAR_FIRST:

time: 52.3 us -> 51.5 us (0.985)
  Pallas kernels: 51.6 us -> 50.8 us
    pallas_call x1, Pallas kernels: 50.1 us -> 49.3 us  [per_device(): pl.pallas_call(kernel, out_shape=(pltpu.VMEM((C, 2, LANES), BF), pltpu.VM...]
where the time goes in v6:
time: 51.5 us; the launch traced here: 51.4 us
  Pallas kernels  50.8 us (99%)
  between operations  0.64 us (1%)
    pallas_call x1, Pallas kernels, per_device(): pl.pallas_call(kernel, out_shape=(pltpu.VMEM((C, 2, LANES), BF), pltpu.VM...  49.3 us
    pallas_call x1, Pallas kernels, per_device(): pl.pallas_call(write_back, out_shape=(jax.ShapeDtypeStruct((C, 2, LANES),...  1.53 us

profile of v6, /device:TPU:1, one launch (start us, length us, event | category | flops | bytes accessed | tf_op | source)
XLA Modules:
  0.0 51.4 jit_solution(15857174898039145456)
XLA Ops:
  0.6 49.3 %shard_map.85 = (bf16[256,2,128]{2,1,0:T(2,128)(2,1)S(1)}, bf16[256,2,128]{2,1,0:T(2,128)(2,1)S(1)}, f32[256,2304]{1,0:T(8,128)S(1)}) custom-call(bf16[256,2,128]{2,1,0:T(2,128)(2,1)} %feat_hbm.1, bf16[256,2,128]{2,1,0:T(2,128)(2,1)} %cot_hbm.1, bf16[256,2304]{1,0:T(8,128)(2,1)} %w_hbm.1, f32[9,5,16]{2,1,0:T(8,128)} %bitcast.3, s32[2,128]{1,0:T(2,128)} %bitcast.5, ...), custom_call_target="tpu_custom_call" | custom-call | tf_op jit(solution)/shard_map/pallas_call | solution.py:445
  49.9 1.5 %shard_map.86 = (bf16[256,2,128]{2,1,0:T(2,128)(2,1)}, bf16[256,2,128]{2,1,0:T(2,128)(2,1)}, f32[256,2304]{1,0:T(8,128)}) custom-call(bf16[256,2,128]{2,1,0:T(2,128)(2,1)S(1)} %get-tuple-element.6.out_v, bf16[256,2,128]{2,1,0:T(2,128)(2,1)S(1)} %get-tuple-element.7.ig_v, f32[256,2304]{1,0:T(8,128)S(1)} %get-tuple-element.8.wg_v), custom_call_target="tpu_custom_call" | custom-call | tf_op jit(solution)/shard_map/pallas_call | solution.py:466

commit v7 on v6

--- a/solution.py
+++ b/solution.py
@@ -299,7 +299,8 @@
             n = from_index(i)
             gx_copy(h, i, n).wait_recv()
             gc_copy(h, i, core).start()
-            widen(h, core, n)
+        for i in NEAR_FIRST:
+            widen(h, core, from_index(i))
 
     def gather_core(h):
         for i in [0] + NEAR_FIRST:

time: 51.5 us -> 51.5 us (level)
  no operation moved by 1% of the time
where the time goes in v7:
time: 51.5 us; the launch traced here: 51.4 us
  Pallas kernels  50.8 us (99%)
  between operations  0.64 us (1%)
    pallas_call x1, Pallas kernels, per_device(): pl.pallas_call(kernel, out_shape=(pltpu.VMEM((C, 2, LANES), BF), pltpu.VM...  49.3 us
    pallas_call x1, Pallas kernels, per_device(): pl.pallas_call(write_back, out_shape=(jax.ShapeDtypeStruct((C, 2, LANES),...  1.53 us

profile of v7, /device:TPU:1, one launch (start us, length us, event | category | flops | bytes accessed | tf_op | source)
XLA Modules:
  0.0 51.4 jit_solution(12061851935329950867)
XLA Ops:
  0.6 49.3 %shard_map.85 = (bf16[256,2,128]{2,1,0:T(2,128)(2,1)S(1)}, bf16[256,2,128]{2,1,0:T(2,128)(2,1)S(1)}, f32[256,2304]{1,0:T(8,128)S(1)}) custom-call(bf16[256,2,128]{2,1,0:T(2,128)(2,1)} %feat_hbm.1, bf16[256,2,128]{2,1,0:T(2,128)(2,1)} %cot_hbm.1, bf16[256,2304]{1,0:T(8,128)(2,1)} %w_hbm.1, f32[9,5,16]{2,1,0:T(8,128)} %bitcast.3, s32[2,128]{1,0:T(2,128)} %bitcast.5, ...), custom_call_target="tpu_custom_call" | custom-call | tf_op jit(solution)/shard_map/pallas_call | solution.py:446
  49.9 1.5 %shard_map.86 = (bf16[256,2,128]{2,1,0:T(2,128)(2,1)}, bf16[256,2,128]{2,1,0:T(2,128)(2,1)}, f32[256,2304]{1,0:T(8,128)}) custom-call(bf16[256,2,128]{2,1,0:T(2,128)(2,1)S(1)} %get-tuple-element.6.out_v, bf16[256,2,128]{2,1,0:T(2,128)(2,1)S(1)} %get-tuple-element.7.ig_v, f32[256,2304]{1,0:T(8,128)S(1)} %get-tuple-element.8.wg_v), custom_call_target="tpu_custom_call" | custom-call | tf_op jit(solution)/shard_map/pallas_call | solution.py:467

commit v8 on v7

--- a/solution.py
+++ b/solution.py
@@ -377,8 +377,8 @@
     acc += dot(edge_hi, sel, TN) + dot(edge_lo, sel, TN)
     ig[...] = lanes_to_rows(acc)
 
+    gather_xy(1)
     gather_core(0)
-    gather_xy(1)
     gather_core(1)
     for i in NEAR_FIRST:
         xy_copy(0, i).wait_send()

time: 51.5 us -> 51.5 us (level)
  no operation moved by 1% of the time
where the time goes in v8:
time: 51.5 us; the launch traced here: 51.4 us
  Pallas kernels  50.8 us (99%)
  between operations  0.64 us (1%)
    pallas_call x1, Pallas kernels, per_device(): pl.pallas_call(kernel, out_shape=(pltpu.VMEM((C, 2, LANES), BF), pltpu.VM...  49.3 us
    pallas_call x1, Pallas kernels, per_device(): pl.pallas_call(write_back, out_shape=(jax.ShapeDtypeStruct((C, 2, LANES),...  1.53 us

profile of v8, /device:TPU:1, one launch (start us, length us, event | category | flops | bytes accessed | tf_op | source)
XLA Modules:
  0.0 51.4 jit_solution(15732950451083248969)
XLA Ops:
  0.6 49.3 %shard_map.85 = (bf16[256,2,128]{2,1,0:T(2,128)(2,1)S(1)}, bf16[256,2,128]{2,1,0:T(2,128)(2,1)S(1)}, f32[256,2304]{1,0:T(8,128)S(1)}) custom-call(bf16[256,2,128]{2,1,0:T(2,128)(2,1)} %feat_hbm.1, bf16[256,2,128]{2,1,0:T(2,128)(2,1)} %cot_hbm.1, bf16[256,2304]{1,0:T(8,128)(2,1)} %w_hbm.1, f32[9,5,16]{2,1,0:T(8,128)} %bitcast.3, s32[2,128]{1,0:T(2,128)} %bitcast.5, ...), custom_call_target="tpu_custom_call" | custom-call | tf_op jit(solution)/shard_map/pallas_call | solution.py:446
  49.9 1.5 %shard_map.86 = (bf16[256,2,128]{2,1,0:T(2,128)(2,1)}, bf16[256,2,128]{2,1,0:T(2,128)(2,1)}, f32[256,2304]{1,0:T(8,128)}) custom-call(bf16[256,2,128]{2,1,0:T(2,128)(2,1)S(1)} %get-tuple-element.6.out_v, bf16[256,2,128]{2,1,0:T(2,128)(2,1)S(1)} %get-tuple-element.7.ig_v, f32[256,2304]{1,0:T(8,128)S(1)} %get-tuple-element.8.wg_v), custom_call_target="tpu_custom_call" | custom-call | tf_op jit(solution)/shard_map/pallas_call | solution.py:467
